TPU v7x, 1024 devices: a whole 4x8x16 slice. The times are simulated.
1024 devices in a mesh: row: 8 (over y_lo, core), col: 128 (over x, y_hi, z).
Axes of the slice: x: 4, y: 8 (y_hi: 2, y_lo: 4; y = y_hi * 4 + y_lo), z: 16, core: 2. Of those that a mesh axis runs over, the one named last changes fastest.
Arguments:
- tiles: float32 [8, 128, 16, 128, 128], P('row', 'col'), may hold values from 0 to 0.01953125
- coords: int32 [8, 128, 2, 16], P('row', 'col'), may hold values from 0 to 31, as said below
- counts: int32 [8, 128], P('row', 'col'), may hold values from 2 to 16
- basis: float32 [32, 524288], P(None, 'col'), may hold values from -6 to 6
Outputs:
- image: float32 [32, 16384], P(None, ('row', 'col'))
- back_image: float32 [32, 524288], P(None, 'col')
Inputs may be any that keep to these rules, and one draw needn't show every extreme that they name: `coords`: within one device the 16 positions are distinct; index 0 is below 16, index 1 below 32.
All inputs are finite; a program needn't handle non-finite values.
Results may differ from a plain program's by a relative error of at most 0.0003.
Values sent between devices are 32-bit elements; how exact they have to be, the bound alone decides.
No kernel may reach another device: no remote copies, remote signals or barrier semaphores. Data moves between devices by JAX's collectives and lax.ppermute only.
A program may use at most 32 MiB of HBM per device.

v0:
```python
import jax
import jax.numpy as jnp
from jax import lax
from jax.sharding import PartitionSpec as P

RT = 16


def per_device(tiles, coords, counts, basis):
    tile_set = tiles[0, 0]
    rows_of = coords[0, 0, 0]
    cols_of = coords[0, 0, 1]
    live_count = counts[0, 0]
    slot_total = tile_set.shape[0]
    tile_edge = tile_set.shape[1]
    block_width = basis.shape[0]
    col_blocks = basis.shape[1] // tile_edge
    row_blocks = RT
    live_mask = (jnp.arange(slot_total, dtype=jnp.int32) < live_count).astype(jnp.float32)
    basis_tiles = basis.reshape(block_width, col_blocks, tile_edge)[:, cols_of, :]
    product = jnp.einsum("sij,ksj->ksi", tile_set, basis_tiles, precision=lax.Precision.HIGHEST)
    product = product * live_mask[None, :, None]
    onehot_rows = (rows_of[:, None] == jnp.arange(row_blocks, dtype=jnp.int32)[None, :]).astype(
        jnp.float32
    )
    partial_value = jnp.einsum("ksi,sr->kri", product, onehot_rows, precision=lax.Precision.HIGHEST)
    partial_value = partial_value.reshape(block_width, row_blocks * tile_edge)
    image_part = lax.psum_scatter(partial_value, "col", scatter_dimension=1, tiled=True)
    image_rows = lax.all_gather(image_part, "col", axis=1, tiled=True)
    image_tiles = image_rows.reshape(block_width, row_blocks, tile_edge)[:, rows_of, :]
    product_back = jnp.einsum(
        "sij,ksi->ksj", tile_set, image_tiles, precision=lax.Precision.HIGHEST
    )
    product_back = product_back * live_mask[None, :, None]
    onehot_cols = (cols_of[:, None] == jnp.arange(col_blocks, dtype=jnp.int32)[None, :]).astype(
        jnp.float32
    )
    back_part = jnp.einsum(
        "ksj,sc->kcj", product_back, onehot_cols, precision=lax.Precision.HIGHEST
    )
    back_part = back_part.reshape(block_width, col_blocks * tile_edge)
    back_image = lax.psum(back_part, "row")
    return (image_part, back_image)


def solution(mesh):
    placed = (
        P("row", "col", None, None, None),
        P("row", "col", None, None),
        P("row", "col"),
        P(None, "col"),
    )
    return jax.shard_map(
        per_device,
        mesh=mesh,
        in_specs=placed,
        out_specs=(P(None, ("row", "col")), P(None, "col")),
        check_vma=False,
    )
```

profile of v0, /device:TPU:1, one launch (start us, length us, event | category | flops | bytes accessed | tf_op | source)
XLA Modules:
  0.0 1422.5 jit_solution(816178794051845927)
XLA Ops:
  7.2 0.0 copy-start
  7.2 0.0 copy-start.1
  7.2 0.0 reduce-scatter.2.cloned.1.call-start
  7.2 0.8 fusion.16
  8.0 0.0 copy-done.1
  8.0 1.1 copy_bitcast_fusion.1
  9.8 0.6 gather_fusion
  10.4 0.0 copy-done
  10.4 1.7 fusion.1
  12.1 0.4 convolution_bitcast_fusion
  12.5 1.3 copy.22
  13.9 0.0 reduce-scatter.2.cloned.1.call-update
  13.9 0.0 all-reduce.2.cloned.1.call-start
  14.0 782.0 %reduce-scatter.2.cloned.1.call-done = f32[32,16]{0,1:T(8,128)} async-done(((f32[32,2048]{0,1:T(8,128)}), f32[32,16]{0,1:T(8,128)}) %reduce-scatter.2.cloned.1.call-update) | async-done | bytes 2064 | tf_op jit(solution)/shard_map/reduce_scatter | solution.py:28
  796.0 377.2 %all_gather.3 = f32[32,2048]{0,1:T(8,128)S(1)} all-gather(f32[32,16]{0,1:T(8,128)} %reduce-scatter.2.cloned.1.call-done), channel_id=1, replica_groups=mesh['row'=8,'col'=128] {'col'}, dimensions={1}, use_global_device_ids=true | all-gather | bytes 264192 | tf_op jit(solution)/shard_map/all_gather | solution.py:29
  1173.2 0.3 copy.20
  1173.5 0.6 gather_fusion.1
  1174.1 1.0 fusion
  1175.1 0.6 fusion.6
  1175.6 1.1 copy.33
  1176.7 0.0 all-reduce.2.cloned.1.call-update
  1176.8 237.0 %all-reduce.2.cloned.1.call-done = f32[32,4096]{1,0:T(8,128)} async-done(((f32[32,4096]{1,0:T(8,128)}), f32[32,4096]{1,0:T(8,128)}) %all-reduce.2.cloned.1.call-update) | async-done | bytes 524304 | tf_op jit(solution)/shard_map/psum | solution.py:42
  1413.8 1.9 copy.36
  (4 shorter events, 0.0 us)
Async XLA Ops:
  7.2 3.2 copy-start
  7.2 0.8 copy-start.1
  7.2 788.8 %reduce-scatter.2.cloned.1.call-start = ((), (), s32[]{:S(2)}) async-start(), calls=%async_computation.1 | async-start | bytes 1056768 | tf_op jit(solution)/shard_map/reduce_scatter | solution.py:28
  13.9 1399.9 %all-reduce.2.cloned.1.call-start = ((), (), s32[]{:S(2)}) async-start(), calls=%async_computation.2 | async-start | bytes 1048576 | tf_op jit(solution)/shard_map/psum | solution.py:42
Sparse Core Ops, SparseCore 0:
  14.0 781.8 reduce-scatter.1
  1176.9 236.8 all-reduce.1
where the time goes:
time: 1420 us
  waiting for transfers between devices  1020 us (72%)
  blocking collectives  377 us (27%)
  between operations  14.8 us (1%)
    reduce_scatter x1, waiting for transfers between devices, per_device(): lax.psum_scatter(partial_value, 'col', scatter_dimension=1, tiled=True)  782 us
    all_gather x1, blocking collectives, per_device(): image_rows = lax.all_gather(image_part, 'col', axis=1, tiled=True)  377 us
    psum x1, waiting for transfers between devices, per_device(): back_image = lax.psum(back_part, 'row')  237 us
  transfers between devices with their start and end apart: 2, of which 2 were waited for; matrix products, arithmetic and copies ran while one was open for 0% of the time, Pallas kernels for 0%

commit v1 on v0

v1 whole, which is shorter than its diff:
```python
import jax
import jax.numpy as jnp
from jax import lax
from jax.experimental import pallas as pl
from jax.experimental.pallas import tpu as pltpu
from jax.sharding import Mesh
from jax.sharding import PartitionSpec as P

K = 32
TILE = 128
RT = 16
CT = 32
SLOTS = 16

AXES = ("yl", "core", "x", "yh", "zh", "zl")
SIZES = (4, 2, 4, 2, 4, 4)
NEAR = ("x", "zl")
FAR = ("yh", "zh")


def split(value):
    high = value.astype(jnp.bfloat16)
    low = (value - high.astype(jnp.float32)).astype(jnp.bfloat16)
    return high, low


def dot3(left, right, contract):
    lh, ll = left
    rh, rl = right
    dims = (((1,), (contract,)), ((), ()))

    def dot(a, b):
        return lax.dot_general(a, b, dims, preferred_element_type=jnp.float32)

    return dot(lh, rh) + (dot(ll, rh) + dot(lh, rl))


def forward_kernel(coords, counts, tiles, basis, part):
    part[...] = jnp.zeros_like(part)
    for s in range(SLOTS):

        @pl.when(s < counts[0])
        def _():
            row = coords[0, s]
            col = pl.multiple_of(coords[1, s] * TILE, TILE)
            part[row] += dot3(split(basis[:, pl.ds(col, TILE)]), split(tiles[s]), 1)


def backward_kernel(coords, counts, core, tiles, image, keep, send, acc):
    acc[...] = jnp.zeros_like(acc)
    for s in range(SLOTS):

        @pl.when(s < counts[0])
        def _():
            row = coords[0, s]
            col = coords[1, s]
            acc[col] += dot3(split(image[row]), split(tiles[s]), 0)

    half = CT // 2
    mine = core[0] * half
    keep[...] = acc[pl.ds(mine, half)]
    send[...] = acc[pl.ds(half - mine, half)]


def sum_copies_kernel(parts, copies):
    total = parts[0]
    for p in range(1, parts.shape[0]):
        total = total + parts[p]
    for p in range(copies.shape[0]):
        copies[p] = total


def join_kernel(core, mine, other, back):
    half = CT // 2
    for j in range(half):
        own = pl.multiple_of((core[0] * half + j) * TILE, TILE)
        far = pl.multiple_of(((1 - core[0]) * half + j) * TILE, TILE)
        back[:, pl.ds(own, TILE)] = mine[j]
        back[:, pl.ds(far, TILE)] = other[j]


SMEM = pl.BlockSpec(memory_space=pltpu.SMEM)
VMEM = pl.BlockSpec(memory_space=pltpu.VMEM)
FLOPS = 2 * SLOTS * K * TILE * TILE


def sum_copies(parts, copies):
    return pl.pallas_call(
        sum_copies_kernel,
        out_shape=jax.ShapeDtypeStruct((copies,) + parts.shape[1:], jnp.float32),
        in_specs=[VMEM],
        out_specs=VMEM,
        cost_estimate=pl.CostEstimate(
            flops=parts.size, bytes_accessed=4 * (parts.size + copies * parts[0].size), transcendentals=0
        ),
    )(parts)


def per_device(tiles, coords, counts, basis):
    tiles = tiles.reshape(SLOTS, TILE, TILE)
    coords = coords.reshape(2, SLOTS)
    counts = counts.reshape(1)
    core = lax.axis_index("core")
    params = pltpu.CompilerParams(vmem_limit_bytes=16 * 1024 * 1024)
    with jax.named_scope("forward"):
        part = pl.pallas_call(
            forward_kernel,
            out_shape=jax.ShapeDtypeStruct((RT, K, TILE), jnp.float32),
            in_specs=[SMEM, SMEM, VMEM, VMEM],
            out_specs=VMEM,
            compiler_params=params,
            cost_estimate=pl.CostEstimate(flops=FLOPS, bytes_accessed=1900000, transcendentals=0),
        )(coords, counts, tiles, basis)
    with jax.named_scope("image_near_sum"):
        got = lax.all_to_all(part, NEAR, 0, 0, tiled=True)
        near = sum_copies(got, 8)
    with jax.named_scope("image_far_sum"):
        got = lax.all_to_all(near, FAR, 0, 0, tiled=True)
        row_tile = sum_copies(got, RT)
    with jax.named_scope("image_gather"):
        image = lax.all_to_all(row_tile, NEAR, 0, 0, tiled=True)
    with jax.named_scope("image_out"):
        index = lax.axis_index(("x", "yh", "zh", "zl"))
        width = RT * TILE // 128
        own = lax.dynamic_slice(
            image, (index // 8, 0, (index % 8) * width), (1, K, width)
        )[0]
    with jax.named_scope("backward"):
        half = jax.ShapeDtypeStruct((CT // 2, K, TILE), jnp.float32)
        keep, send = pl.pallas_call(
            backward_kernel,
            out_shape=[half, half],
            in_specs=[SMEM, SMEM, SMEM, VMEM, VMEM],
            out_specs=[VMEM, VMEM],
            scratch_shapes=[pltpu.VMEM((CT, K, TILE), jnp.float32)],
            compiler_params=params,
            cost_estimate=pl.CostEstimate(flops=FLOPS, bytes_accessed=1900000, transcendentals=0),
        )(coords, counts, core.reshape(1), tiles, image)
    swap = [(0, 1), (1, 0)]
    with jax.named_scope("back_core_sum"):
        both = keep + lax.ppermute(send, "core", swap)
    with jax.named_scope("back_row_sum"):
        got = lax.all_to_all(both, "yl", 0, 0, tiled=True)
        quarter = sum_copies(got.reshape(4, 4 * K, TILE), 4)
    with jax.named_scope("back_row_gather"):
        mine = lax.all_to_all(quarter.reshape(CT // 2, K, TILE), "yl", 0, 0, tiled=True)
    with jax.named_scope("back_core_gather"):
        other = lax.ppermute(mine, "core", swap)
        back = pl.pallas_call(
            join_kernel,
            out_shape=jax.ShapeDtypeStruct((K, CT * TILE), jnp.float32),
            in_specs=[SMEM, VMEM, VMEM],
            out_specs=VMEM,
            cost_estimate=pl.CostEstimate(flops=0, bytes_accessed=1100000, transcendentals=0),
        )(core.reshape(1), mine, other)
    return own, back


def solution(mesh):
    fine = Mesh(mesh.devices.reshape(SIZES), AXES)
    row = ("yl", "core")
    col = ("x", "yh", "zh", "zl")
    return jax.shard_map(
        per_device,
        mesh=fine,
        in_specs=(
            P(row, col, None, None, None),
            P(row, col, None, None),
            P(row, col),
            P(None, col),
        ),
        out_specs=(P(None, row + col), P(None, col)),
        check_vma=False,
    )
```

time: 1420 us -> 123 us (0.09)
  waiting for transfers between devices: 1020 us -> 9.48 us
  blocking collectives: 377 us -> 80.1 us
  starting transfers between devices: 0.08 us -> 16.3 us
    reduce_scatter x1 -> x0, waiting for transfers between devices: 782 us -> none  [per_device(): lax.psum_scatter(partial_value, 'col', scatter_dimension=1, tiled=True)]
    all_gather x1 -> x0, blocking collectives: 377 us -> none  [per_device(): image_rows = lax.all_gather(image_part, 'col', axis=1, tiled=True)]
    psum x1 -> x0, waiting for transfers between devices: 237 us -> none  [per_device(): back_image = lax.psum(back_part, 'row')]
    all_to_all x0 -> x4, blocking collectives: none -> 80.1 us  [the longest x1 38.8 us: per_device(): got = lax.all_to_all(near, FAR, 0, 0, tiled=True)]
  transfers between devices with their start and end apart: 2 -> 3, of which waited for: 2 -> 3; matrix products, arithmetic and copies ran while one was open for 0% -> 1% of each run, Pallas kernels for 0% -> 0%
where the time goes in v1:
time: 123 us; the launch traced here: 122 us
  blocking collectives  80.1 us (65%)
  starting transfers between devices  16.3 us (13%)
  Pallas kernels  10.6 us (9%)
  waiting for transfers between devices  9.48 us (8%)
  local copies, waits for them, and re-layouts  4.4 us (4%)
  between operations  1.39 us (1%)
    all_to_all x1, blocking collectives, per_device(): got = lax.all_to_all(near, FAR, 0, 0, tiled=True)  38.8 us
    all_to_all x1, blocking collectives, per_device(): got = lax.all_to_all(part, NEAR, 0, 0, tiled=True)  19.7 us
    all_to_all x1, blocking collectives, per_device(): got = lax.all_to_all(both, 'yl', 0, 0, tiled=True)  11.1 us
    all_to_all x1, blocking collectives, per_device(): lax.all_to_all(quarter.reshape(CT // 2, K, TILE), 'yl', 0, 0, tiled=True)  10.7 us
    all_to_all x1, waiting for transfers between devices, per_device(): image = lax.all_to_all(row_tile, NEAR, 0, 0, tiled=True)  7.98 us
    ppermute x1, starting transfers between devices, per_device(): both = keep + lax.ppermute(send, 'core', swap)  6.19 us
    ppermute x1, starting transfers between devices, per_device(): other = lax.ppermute(mine, 'core', swap)  5.66 us
    pallas_call x3, Pallas kernels, sum_copies(): pl.pallas_call(sum_copies_kernel, out_shape=jax.ShapeDtypeStruct((copies,...  4.94 us
  transfers between devices with their start and end apart: 3, of which 3 were waited for; matrix products, arithmetic and copies ran while one was open for 1% of the time, Pallas kernels for 0%

profile of v1, /device:TPU:1, one launch (start us, length us, event | category | flops | bytes accessed | tf_op | source)
XLA Modules:
  0.0 122.4 jit_solution(2027474666985531217)
XLA Ops:
  1.3 0.0 copy-start.3
  1.3 0.7 copy-done.3
  2.0 0.0 copy-start
  2.0 1.2 copy-done
  3.2 0.0 copy-start.2
  3.2 1.0 copy-done.2
  4.2 2.0 %forward.1 = f32[16,32,128]{2,1,0:T(8,128)S(1)} custom-call(s32[2,16]{1,0:T(2,128)S(1)} %bitcast.11, s32[1]{0:T(128)} %bitcast.7.counts, f32[16,128,128]{2,1,0:T(8,128)S(1)} %bitcast.9, f32[32,4096]{1,0:T(8,128)S(1)} %copy-done.2), custom_call_target="tpu_custom_call" | custom-call | flops 16777216 | bytes 1900000 | tf_op jit(solution)/shard_map/forward/pallas_call | solution.py:106
  6.2 0.0 copy-start.1
  6.2 19.7 %all_to_all.25.parts = f32[16,32,128]{2,1,0:T(8,128)} all-to-all(f32[16,32,128]{2,1,0:T(8,128)S(1)} %forward.1), channel_id=1, replica_groups=mesh['yl'=4,'core'=2,'x'=4,'yh'=2,'zh'=4,'zl'=4] {'x','zl'}, dimensions={0} | all-to-all | bytes 524288 | tf_op jit(solution)/shard_map/image_near_sum/all_to_all | solution.py:115
  25.9 1.6 %image_near_sum.1 = f32[8,32,128]{2,1,0:T(8,128)} custom-call(f32[16,32,128]{2,1,0:T(8,128)} %all_to_all.25.parts), custom_call_target="tpu_custom_call" | custom-call | flops 65536 | bytes 393216 | tf_op jit(solution)/shard_map/image_near_sum/pallas_call | solution.py:88
  27.5 38.8 %all_to_all.26.parts = f32[8,32,128]{2,1,0:T(8,128)} all-to-all(f32[8,32,128]{2,1,0:T(8,128)} %image_near_sum.1), channel_id=1, replica_groups=mesh['yl'=4,'core'=2,'x'=4,'yh'=2,'zh'=4,'zl'=4] {'yh','zh'}, dimensions={0} | all-to-all | bytes 262144 | tf_op jit(solution)/shard_map/image_far_sum/all_to_all | solution.py:118
  66.3 1.6 %image_far_sum.1 = f32[16,32,128]{2,1,0:T(8,128)} custom-call(f32[8,32,128]{2,1,0:T(8,128)} %all_to_all.26.parts), custom_call_target="tpu_custom_call" | custom-call | flops 32768 | bytes 393216 | tf_op jit(solution)/shard_map/image_far_sum/pallas_call | solution.py:88
  67.9 4.5 %all-to-all-start.2 = ((f32[16,32,128]{2,1,0:T(8,128)}), f32[16,32,128]{2,1,0:T(8,128)S(1)}, u32[]{:S(2)}, u32[]{:S(2)}) async-start(f32[16,32,128]{2,1,0:T(8,128)} %image_far_sum.1), calls=%async_computation.2 | async-start | bytes 524288 | tf_op jit(solution)/shard_map/image_gather/all_to_all | solution.py:121
  72.4 8.0 %all-to-all-done.2.image = f32[16,32,128]{2,1,0:T(8,128)S(1)} async-done(((f32[16,32,128]{2,1,0:T(8,128)}), f32[16,32,128]{2,1,0:T(8,128)S(1)}, u32[]{:S(2)}, u32[]{:S(2)}) %all-to-all-start.2) | async-done | bytes 262176 | tf_op jit(solution)/shard_map/image_gather/all_to_all | solution.py:121
  80.4 0.0 copy-done.1
  80.4 1.8 %backward.1 = (f32[16,32,128]{2,1,0:T(8,128)S(1)}, f32[16,32,128]{2,1,0:T(8,128)S(1)}) custom-call(s32[2,16]{1,0:T(2,128)S(1)} %bitcast.12, s32[1]{0:T(128)} %bitcast.8.counts, s32[1]{0:T(128)} %bitcast.4.core, f32[16,128,128]{2,1,0:T(8,128)S(1)} %bitcast.10, f32[16,32,128]{2,1,0:T(8,128)S(1)} %all-to-all-done.2.image), custom_call_target="tpu_custom_call" | custom-call | flops 16777216 | bytes 1900000 | tf_op jit(solution)/shard_map/backward/pallas_call | solution.py:130
  82.2 6.2 %collective-permute-start = (f32[16,32,128]{2,1,0:T(8,128)S(1)}, f32[16,32,128]{2,1,0:T(8,128)S(1)}, u32[]{:S(2)}, u32[]{:S(2)}) collective-permute-start(f32[16,32,128]{2,1,0:T(8,128)S(1)} %get-tuple-element.5), channel_id=1, source_target_pairs={{0,128},{128,0},{1,129},{129,1},{2,130},{130,2},{3,131},{131,3},{4... | collective-permute-start | bytes 786440 | tf_op jit(solution)/shard_map/back_core_sum/ppermute | solution.py:141
  88.4 1.1 collective-permute-done
  89.6 11.1 %all_to_all.27 = f32[16,32,128]{2,1,0:T(8,128)} all-to-all(f32[16,32,128]{2,1,0:T(8,128)S(1)} %add.29), channel_id=1, replica_groups=mesh['yl'=4,'core'=2,'x'=4,'yh'=2,'zh'=4,'zl'=4] {'yl'}, dimensions={0} | all-to-all | bytes 524288 | tf_op jit(solution)/shard_map/back_row_sum/all_to_all | solution.py:143
  100.6 1.7 %back_row_sum.1 = f32[4,128,128]{2,1,0:T(8,128)} custom-call(f32[4,128,128]{2,1,0:T(8,128)} %bitcast.13), custom_call_target="tpu_custom_call" | custom-call | flops 65536 | bytes 524288 | tf_op jit(solution)/shard_map/back_row_sum/pallas_call | solution.py:88
  102.3 10.7 %all_to_all.28.mine = f32[16,32,128]{2,1,0:T(8,128)S(1)} all-to-all(f32[16,32,128]{2,1,0:T(8,128)} %bitcast.14), channel_id=1, replica_groups=mesh['yl'=4,'core'=2,'x'=4,'yh'=2,'zh'=4,'zl'=4] {'yl'}, dimensions={0} | all-to-all | bytes 524288 | tf_op jit(solution)/shard_map/back_row_gather/all_to_all | solution.py:146
  113.0 0.0 copy-start.4
  113.0 5.7 %collective-permute-start.1 = (f32[16,32,128]{2,1,0:T(8,128)S(1)}, f32[16,32,128]{2,1,0:T(8,128)S(1)}, u32[]{:S(2)}, u32[]{:S(2)}) collective-permute-start(f32[16,32,128]{2,1,0:T(8,128)S(1)} %all_to_all.28.mine), channel_id=1, source_target_pairs={{0,128},{128,0},{1,129},{129,1},{2,130},{130,2},{3,131},{131,3},{4... | collective-permute-start | bytes 786440 | tf_op jit(solution)/shard_map/back_core_gather/ppermute | solution.py:148
  118.7 0.1 constant_dynamic-slice_fusion
  118.8 0.7 copy.6
  119.4 0.4 collective-permute-done.1.other
  119.8 0.0 copy-done.4
  119.8 0.0 copy-start.5
  119.8 0.7 copy-done.5
  120.5 1.9 %back_core_gather.1 = f32[32,4096]{1,0:T(8,128)} custom-call(s32[1]{0:T(128)} %bitcast.4.core, f32[16,32,128]{2,1,0:T(8,128)} %copy-done.4, f32[16,32,128]{2,1,0:T(8,128)} %copy-done.5), custom_call_target="tpu_custom_call" | custom-call | bytes 1100000 | tf_op jit(solution)/shard_map/back_core_gather/pallas_call | solution.py:149
  (1 shorter events, 0.0 us)
Async XLA Ops:
  1.3 0.7 copy-start.3
  2.0 1.2 %copy-start = (f32[1,1,16,128,128]{4,3,2,1,0:T(8,128)S(1)}, f32[1,1,16,128,128]{4,3,2,1,0:T(8,128)}, u32[]{:S(2)}) copy-start(f32[1,1,16,128,128]{4,3,2,1,0:T(8,128)} %param.4) | copy-start | bytes 3145732
  3.2 1.0 copy-start.2
  6.2 74.2 %copy-start.1 = (f32[1,1,16,128,128]{4,3,2,1,0:T(8,128)S(1)}, f32[1,1,16,128,128]{4,3,2,1,0:T(8,128)}, u32[]{:S(2)}) copy-start(f32[1,1,16,128,128]{4,3,2,1,0:T(8,128)} %param.4) | copy-start | bytes 3145732
  67.9 12.5 %all-to-all-start.2 = ((f32[16,32,128]{2,1,0:T(8,128)}), f32[16,32,128]{2,1,0:T(8,128)S(1)}, u32[]{:S(2)}, u32[]{:S(2)}) async-start(f32[16,32,128]{2,1,0:T(8,128)} %image_far_sum.1), calls=%async_computation.2 | async-start | bytes 524288 | tf_op jit(solution)/shard_map/image_gather/all_to_all | solution.py:121
  82.2 7.3 %collective-permute-start = (f32[16,32,128]{2,1,0:T(8,128)S(1)}, f32[16,32,128]{2,1,0:T(8,128)S(1)}, u32[]{:S(2)}, u32[]{:S(2)}) collective-permute-start(f32[16,32,128]{2,1,0:T(8,128)S(1)} %get-tuple-element.5), channel_id=1, source_target_pairs={{0,128},{128,0},{1,129},{129,1},{2,130},{130,2},{3,131},{131,3},{4... | collective-permute-start | bytes 786440 | tf_op jit(solution)/shard_map/back_core_sum/ppermute | solution.py:141
  113.0 6.8 %copy-start.4 = (f32[16,32,128]{2,1,0:T(8,128)}, f32[16,32,128]{2,1,0:T(8,128)S(1)}, u32[]{:S(2)}) copy-start(f32[16,32,128]{2,1,0:T(8,128)S(1)} %all_to_all.28.mine) | copy-start | bytes 786436
  113.0 6.8 %collective-permute-start.1 = (f32[16,32,128]{2,1,0:T(8,128)S(1)}, f32[16,32,128]{2,1,0:T(8,128)S(1)}, u32[]{:S(2)}, u32[]{:S(2)}) collective-permute-start(f32[16,32,128]{2,1,0:T(8,128)S(1)} %all_to_all.28.mine), channel_id=1, source_target_pairs={{0,128},{128,0},{1,129},{129,1},{2,130},{130,2},{3,131},{131,3},{4... | collective-permute-start | bytes 786440 | tf_op jit(solution)/shard_map/back_core_gather/ppermute | solution.py:148
  119.8 0.7 copy-start.5

commit v2 on v1

v2 whole, which is shorter than its diff:
```python
import jax
import jax.numpy as jnp
from jax import lax
from jax.experimental import pallas as pl
from jax.experimental.pallas import tpu as pltpu
from jax.sharding import Mesh
from jax.sharding import PartitionSpec as P

K = 32
TILE = 128
RT = 16
CT = 32
SLOTS = 16
GROUP = 4

AXES = ("yl", "core", "x", "yh", "zh", "zl")
SIZES = (4, 2, 4, 2, 4, 4)
NEAR = ("x", "zl")
FAR = ("yh", "zh")


def split(value):
    high = value.astype(jnp.bfloat16)
    low = (value - high.astype(jnp.float32)).astype(jnp.bfloat16)
    return high, low


def dot3(left, right_high, right_low, contract):
    high, low = split(left)
    dims = (((1,), (contract,)), ((), ()))
    both = lax.dot_general(
        jnp.concatenate([high, low], axis=0), right_high, dims, preferred_element_type=jnp.float32
    )
    rest = lax.dot_general(high, right_low, dims, preferred_element_type=jnp.float32)
    rows = left.shape[0]
    return both[:rows] + (both[rows:] + rest)


def forward_kernel(
    counts, coords_in, tiles_in, basis_in, part, high, low, coords_out, coords, tiles, basis, small, wide, slots
):
    copies = [
        pltpu.make_async_copy(coords_in, coords, small.at[0]),
        pltpu.make_async_copy(coords_in, coords_out, small.at[1]),
    ]
    for p in range(4):
        rows = pl.ds(p * (K // 4), K // 4)
        copies.append(pltpu.make_async_copy(basis_in.at[rows], basis.at[rows], wide.at[p]))
    for copy in copies:
        copy.start()
    landed = [pltpu.make_async_copy(tiles_in.at[s], tiles.at[s], slots.at[s]) for s in range(SLOTS)]
    for copy in landed:
        copy.start()
    part[...] = jnp.zeros_like(part)
    for copy in copies:
        copy.wait()
    live = counts[0]
    for first in range(0, SLOTS, GROUP):
        for s in range(first, first + GROUP):
            landed[s].wait()

        @pl.when(first < live)
        def _():
            for s in range(first, first + GROUP):
                high[s], low[s] = split(tiles[s])
            for s in range(first, first + GROUP):
                row = coords[0, s]
                col = pl.multiple_of(coords[1, s] * TILE, TILE)
                product = dot3(basis[:, pl.ds(col, TILE)], high[s], low[s], 1)
                part[row] += jnp.where(s < live, product, 0.0)


def backward_kernel(coords, counts, core, high, low, image, keep, send, acc):
    acc[...] = jnp.zeros_like(acc)
    live = counts[0]
    for first in range(0, SLOTS, GROUP):

        @pl.when(first < live)
        def _():
            for s in range(first, first + GROUP):
                product = dot3(image[coords[0, s]], high[s], low[s], 0)
                acc[coords[1, s]] += jnp.where(s < live, product, 0.0)

    half = CT // 2
    mine = core[0, 0] * half
    keep[...] = acc[pl.ds(mine, half)]
    send[...] = acc[pl.ds(half - mine, half)]


def sum_copies_kernel(parts, copies):
    total = parts[0]
    for p in range(1, parts.shape[0]):
        total = total + parts[p]
    for p in range(copies.shape[0]):
        copies[p] = total


def place_kernel(core_xor, part, *refs):
    back, sems = refs[-2:]
    first = core_xor[0, 0]
    half = CT // 2
    copies = []
    for j in range(half):
        column = pl.multiple_of((first * half + j) * TILE, TILE)
        copies.append(pltpu.make_async_copy(part.at[j], back.at[:, pl.ds(column, TILE)], sems.at[j]))
    for copy in copies:
        copy.start()
    for copy in copies:
        copy.wait()


SMEM = pl.BlockSpec(memory_space=pltpu.SMEM)
VMEM = pl.BlockSpec(memory_space=pltpu.VMEM)
ANY = pl.BlockSpec(memory_space=pl.ANY)
MIB = 1024 * 1024
FLOPS = 2 * SLOTS * K * TILE * TILE


def sum_copies(parts, copies):
    return pl.pallas_call(
        sum_copies_kernel,
        out_shape=pltpu.VMEM((copies,) + parts.shape[1:], jnp.float32),
        in_specs=[VMEM],
        out_specs=VMEM,
        compiler_params=pltpu.CompilerParams(vmem_limit_bytes=2 * MIB),
        cost_estimate=pl.CostEstimate(
            flops=parts.size, bytes_accessed=4 * (parts.size + copies * parts[0].size), transcendentals=0
        ),
    )(parts)


def lane(value):
    return jnp.broadcast_to(value, (8, TILE))


def place(core, part, *back):
    return pl.pallas_call(
        place_kernel,
        out_shape=jax.ShapeDtypeStruct((K, CT * TILE), jnp.float32),
        in_specs=[VMEM, ANY] + [ANY] * len(back),
        out_specs=ANY,
        scratch_shapes=[pltpu.SemaphoreType.DMA((CT // 2,))],
        input_output_aliases={2: 0} if back else {},
        compiler_params=pltpu.CompilerParams(vmem_limit_bytes=2 * MIB),
        cost_estimate=pl.CostEstimate(flops=0, bytes_accessed=600000, transcendentals=0),
    )(core, part, *back)


def per_device(tiles, coords, counts, basis):
    tiles = tiles.reshape(SLOTS, TILE, TILE)
    coords = coords.reshape(2, SLOTS)
    counts = counts.reshape(1)
    index = lax.axis_index(("x", "yh", "zh", "zl"))
    core = lax.axis_index("core")
    width = RT * TILE // 128
    spots = (index // 8, index % 8 * width, lane(core), lane(1 - core))
    params = pltpu.CompilerParams(vmem_limit_bytes=8 * MIB)
    halves = jax.ShapeDtypeStruct((SLOTS, TILE, TILE), jnp.bfloat16)
    with jax.named_scope("forward"):
        part, high, low, places = pl.pallas_call(
            forward_kernel,
            out_shape=[
                jax.ShapeDtypeStruct((RT, K, TILE), jnp.float32),
                halves,
                halves,
                jax.ShapeDtypeStruct((2, SLOTS), jnp.int32),
            ],
            in_specs=[SMEM] + [ANY] * 3,
            out_specs=[VMEM] * 4,
            scratch_shapes=[
                pltpu.SMEM((2, SLOTS), jnp.int32),
                pltpu.VMEM((SLOTS, TILE, TILE), jnp.float32),
                pltpu.VMEM((K, CT * TILE), jnp.float32),
                pltpu.SemaphoreType.DMA((2,)),
                pltpu.SemaphoreType.DMA((4,)),
                pltpu.SemaphoreType.DMA((SLOTS,)),
            ],
            compiler_params=params,
            cost_estimate=pl.CostEstimate(flops=FLOPS, bytes_accessed=1900000, transcendentals=0),
        )(counts, *[pltpu.with_memory_space_constraint(a, pltpu.HBM) for a in (coords, tiles, basis)])
    with jax.named_scope("image_near_sum"):
        got = lax.all_to_all(part, NEAR, 0, 0, tiled=True)
        near = sum_copies(got, 8)
    with jax.named_scope("image_far_sum"):
        got = lax.all_to_all(near, FAR, 0, 0, tiled=True)
        got, counts, *spots = lax.optimization_barrier((got, counts) + spots)
        own_tile, own_column, core_lane, other_lane = spots
        row_tile = sum_copies(got, RT)
    with jax.named_scope("image_gather"):
        image = lax.all_to_all(row_tile, NEAR, 0, 0, tiled=True)
    with jax.named_scope("image_out"):
        own = lax.dynamic_slice(image, (own_tile, 0, own_column), (1, K, width))[0]
    with jax.named_scope("backward"):
        half = jax.ShapeDtypeStruct((CT // 2, K, TILE), jnp.float32)
        keep, send = pl.pallas_call(
            backward_kernel,
            out_shape=[half, half],
            in_specs=[SMEM, SMEM, VMEM, VMEM, VMEM, VMEM],
            out_specs=[VMEM, VMEM],
            scratch_shapes=[pltpu.VMEM((CT, K, TILE), jnp.float32)],
            compiler_params=params,
            cost_estimate=pl.CostEstimate(flops=FLOPS, bytes_accessed=1900000, transcendentals=0),
        )(places, counts, core_lane, high, low, image)
    swap = [(0, 1), (1, 0)]
    with jax.named_scope("back_core_sum"):
        theirs, own = lax.optimization_barrier((lax.ppermute(send, "core", swap), own))
        both = keep + theirs
    with jax.named_scope("back_row_sum"):
        got = lax.all_to_all(both, "yl", 0, 0, tiled=True)
        quarter = sum_copies(got.reshape(4, 4 * K, TILE), 4)
    with jax.named_scope("back_row_gather"):
        mine = lax.all_to_all(quarter.reshape(CT // 2, K, TILE), "yl", 0, 0, tiled=True)
    with jax.named_scope("back_core_gather"):
        other = lax.ppermute(mine, "core", swap)
        back = place(core_lane, mine)
        back = place(other_lane, other, back)
    return own, back


def solution(mesh):
    fine = Mesh(mesh.devices.reshape(SIZES), AXES)
    row = ("yl", "core")
    col = ("x", "yh", "zh", "zl")
    return jax.shard_map(
        per_device,
        mesh=fine,
        in_specs=(
            P(row, col, None, None, None),
            P(row, col, None, None),
            P(row, col),
            P(None, col),
        ),
        out_specs=(P(None, row + col), P(None, col)),
        check_vma=False,
    )
```

time: 123 us -> 111 us (0.902)
  blocking collectives: 80.1 us -> 50.1 us
  starting transfers between devices: 16.3 us -> 36.5 us
  waiting for transfers between devices: 9.48 us -> 17.2 us
  Pallas kernels: 10.6 us -> 5.2 us
  local copies, waits for them, and re-layouts: 4.4 us -> 0.75 us
    all_to_all x1, blocking collectives: 38.8 us -> 12.1 us  [per_device(): image = lax.all_to_all(row_tile, NEAR, 0, 0, tiled=True)]
    all_to_all x1, starting transfers between devices: 4.46 us -> 23.6 us  [per_device(): got = lax.all_to_all(near, FAR, 0, 0, tiled=True)]
    all_to_all x1, waiting for transfers between devices: 7.98 us -> 16.5 us  [per_device(): got = lax.all_to_all(near, FAR, 0, 0, tiled=True)]
    pallas_call x5 -> x6, Pallas kernels: 8.79 us -> 4.39 us  [the longest x1 1.94 us: per_device(): pl.pallas_call(forward_kernel, out_shape=[jax.ShapeDtypeStruct((RT, K, TI...]
    unnamed x12 -> x0, local copies, waits for them, and re-layouts: 3.65 us -> none
    all_to_all x1, blocking collectives: 10.7 us -> 8.81 us  [per_device(): lax.all_to_all(quarter.reshape(CT // 2, K, TILE), 'yl', 0, 0, tiled=True)]
  transfers between devices with their start and end apart: 3 -> 3, of which waited for: 3 -> 3; matrix products, arithmetic and copies ran while one was open for 1% -> 1% of each run, Pallas kernels for 0% -> 1%
where the time goes in v2:
time: 111 us
  blocking collectives  50.1 us (45%)
  starting transfers between devices  36.5 us (33%)
  waiting for transfers between devices  17.2 us (15%)
  Pallas kernels  5.2 us (5%)
  between operations  1.35 us (1%)
    all_to_all x1, starting transfers between devices, per_device(): got = lax.all_to_all(near, FAR, 0, 0, tiled=True)  23.6 us
    all_to_all x1, blocking collectives, per_device(): got = lax.all_to_all(part, NEAR, 0, 0, tiled=True)  18.5 us
    all_to_all x1, waiting for transfers between devices, per_device(): got = lax.all_to_all(near, FAR, 0, 0, tiled=True)  16.5 us
    all_to_all x1, blocking collectives, per_device(): image = lax.all_to_all(row_tile, NEAR, 0, 0, tiled=True)  12.1 us
    all_to_all x1, blocking collectives, per_device(): got = lax.all_to_all(both, 'yl', 0, 0, tiled=True)  10.7 us
    all_to_all x1, blocking collectives, per_device(): lax.all_to_all(quarter.reshape(CT // 2, K, TILE), 'yl', 0, 0, tiled=True)  8.81 us
    ppermute x1, starting transfers between devices, per_device(): lax.ppermute(send, 'core', swap)  7.22 us
    ppermute x1, starting transfers between devices, per_device(): other = lax.ppermute(mine, 'core', swap)  5.66 us
  transfers between devices with their start and end apart: 3, of which 3 were waited for; matrix products, arithmetic and copies ran while one was open for 1% of the time, Pallas kernels for 1%

profile of v2, /device:TPU:1, one launch (start us, length us, event | category | flops | bytes accessed | tf_op | source)
XLA Modules:
  0.0 111.1 jit_solution(15999649288312297224)
XLA Ops:
  1.3 1.9 %forward.1 = (f32[16,32,128]{2,1,0:T(8,128)S(1)}, bf16[16,128,128]{2,1,0:T(8,128)(2,1)S(1)}, bf16[16,128,128]{2,1,0:T(8,128)(2,1)S(1)}, s32[2,16]{1,0:T(2,128)S(1)}) custom-call(s32[1]{0:T(128)} %bitcast.7.counts, s32[2,16]{1,0:T(2,128)} %bitcast.12, f32[16,128,128]{2,1,0:T(8,128)} %bitcast.10, f32[32,4096]{1,0:T(8,128)} %basis_in.1), custom_call_target="tpu_custom_call" | custom-call | flops 16777216 | bytes 1900000 | tf_op jit(solution)/shard_map/forward/pallas_call | solution.py:160
  3.2 18.5 %all_to_all.25.parts = f32[16,32,128]{2,1,0:T(8,128)S(1)} all-to-all(f32[16,32,128]{2,1,0:T(8,128)S(1)} %get-tuple-element.17), channel_id=1, replica_groups=mesh['yl'=4,'core'=2,'x'=4,'yh'=2,'zh'=4,'zl'=4] {'x','zl'}, dimensions={0} | all-to-all | bytes 524288 | tf_op jit(solution)/shard_map/image_near_sum/all_to_all | solution.py:182
  21.7 0.7 image_near_sum.1
  22.4 23.6 %all-to-all-start.1 = ((f32[8,32,128]{2,1,0:T(8,128)}), f32[8,32,128]{2,1,0:T(8,128)S(1)}, u32[]{:S(2)}, u32[]{:S(2)}) async-start(f32[8,32,128]{2,1,0:T(8,128)} %image_near_sum.1), calls=%async_computation.1 | async-start | bytes 262144 | tf_op jit(solution)/shard_map/image_far_sum/all_to_all | solution.py:185
  46.0 16.5 %all-to-all-done.1.parts = f32[8,32,128]{2,1,0:T(8,128)S(1)} async-done(((f32[8,32,128]{2,1,0:T(8,128)}), f32[8,32,128]{2,1,0:T(8,128)S(1)}, u32[]{:S(2)}, u32[]{:S(2)}) %all-to-all-start.1) | async-done | bytes 131104 | tf_op jit(solution)/shard_map/image_far_sum/all_to_all | solution.py:185
  62.5 12.1 %all_to_all.26.image = f32[16,32,128]{2,1,0:T(8,128)S(1)} all-to-all(f32[16,32,128]{2,1,0:T(8,128)S(1)} %image_far_sum.1), channel_id=1, replica_groups=mesh['yl'=4,'core'=2,'x'=4,'yh'=2,'zh'=4,'zl'=4] {'x','zl'}, dimensions={0} | all-to-all | bytes 524288 | tf_op jit(solution)/shard_map/image_gather/all_to_all | solution.py:190
  74.7 0.8 backward.1
  75.5 7.2 %collective-permute-start = (f32[16,32,128]{2,1,0:T(8,128)S(1)}, f32[16,32,128]{2,1,0:T(8,128)S(1)}, u32[]{:S(2)}, u32[]{:S(2)}) collective-permute-start(f32[16,32,128]{2,1,0:T(8,128)S(1)} %get-tuple-element.23), channel_id=1, source_target_pairs={{0,128},{128,0},{1,129},{129,1},{2,130},{130,2},{3,131},{131,3},{4... | collective-permute-start | bytes 786440 | tf_op jit(solution)/shard_map/back_core_sum/ppermute | solution.py:206
  82.7 0.1 constant_dynamic-slice_fusion
  82.8 0.7 copy.7
  83.5 0.4 collective-permute-done
  83.9 10.7 %all_to_all.27 = f32[16,32,128]{2,1,0:T(8,128)S(1)} all-to-all(f32[16,32,128]{2,1,0:T(8,128)S(1)} %add.29), channel_id=1, replica_groups=mesh['yl'=4,'core'=2,'x'=4,'yh'=2,'zh'=4,'zl'=4] {'yl'}, dimensions={0} | all-to-all | bytes 524288 | tf_op jit(solution)/shard_map/back_row_sum/all_to_all | solution.py:209
  94.6 8.8 %all_to_all.28.part = f32[16,32,128]{2,1,0:T(8,128)S(1)} all-to-all(f32[16,32,128]{2,1,0:T(8,128)S(1)} %bitcast.9), channel_id=1, replica_groups=mesh['yl'=4,'core'=2,'x'=4,'yh'=2,'zh'=4,'zl'=4] {'yl'}, dimensions={0} | all-to-all | bytes 524288 | tf_op jit(solution)/shard_map/back_row_gather/all_to_all | solution.py:212
  103.4 5.7 %collective-permute-start.1 = (f32[16,32,128]{2,1,0:T(8,128)S(1)}, f32[16,32,128]{2,1,0:T(8,128)S(1)}, u32[]{:S(2)}, u32[]{:S(2)}) collective-permute-start(f32[16,32,128]{2,1,0:T(8,128)S(1)} %all_to_all.28.part), channel_id=1, source_target_pairs={{0,128},{128,0},{1,129},{129,1},{2,130},{130,2},{3,131},{131,3},{4... | collective-permute-start | bytes 786440 | tf_op jit(solution)/shard_map/back_core_gather/ppermute | solution.py:214
  109.0 0.9 back_core_gather.2.refs_0_
  109.9 0.3 collective-permute-done.1.part
  110.2 0.9 back_core_gather.3
  (5 shorter events, 0.1 us)
Async XLA Ops:
  22.4 40.1 %all-to-all-start.1 = ((f32[8,32,128]{2,1,0:T(8,128)}), f32[8,32,128]{2,1,0:T(8,128)S(1)}, u32[]{:S(2)}, u32[]{:S(2)}) async-start(f32[8,32,128]{2,1,0:T(8,128)} %image_near_sum.1), calls=%async_computation.1 | async-start | bytes 262144 | tf_op jit(solution)/shard_map/image_far_sum/all_to_all | solution.py:185
  75.5 8.4 %collective-permute-start = (f32[16,32,128]{2,1,0:T(8,128)S(1)}, f32[16,32,128]{2,1,0:T(8,128)S(1)}, u32[]{:S(2)}, u32[]{:S(2)}) collective-permute-start(f32[16,32,128]{2,1,0:T(8,128)S(1)} %get-tuple-element.23), channel_id=1, source_target_pairs={{0,128},{128,0},{1,129},{129,1},{2,130},{130,2},{3,131},{131,3},{4... | collective-permute-start | bytes 786440 | tf_op jit(solution)/shard_map/back_core_sum/ppermute | solution.py:206
  103.4 6.8 %collective-permute-start.1 = (f32[16,32,128]{2,1,0:T(8,128)S(1)}, f32[16,32,128]{2,1,0:T(8,128)S(1)}, u32[]{:S(2)}, u32[]{:S(2)}) collective-permute-start(f32[16,32,128]{2,1,0:T(8,128)S(1)} %all_to_all.28.part), channel_id=1, source_target_pairs={{0,128},{128,0},{1,129},{129,1},{2,130},{130,2},{3,131},{131,3},{4... | collective-permute-start | bytes 786440 | tf_op jit(solution)/shard_map/back_core_gather/ppermute | solution.py:214

commit v3 on v2

--- a/solution.py
+++ b/solution.py
@@ -3,7 +3,6 @@
 from jax import lax
 from jax.experimental import pallas as pl
 from jax.experimental.pallas import tpu as pltpu
-from jax.sharding import Mesh
 from jax.sharding import PartitionSpec as P
 
 K = 32
@@ -13,10 +12,33 @@
 SLOTS = 16
 GROUP = 4
 
-AXES = ("yl", "core", "x", "yh", "zh", "zl")
-SIZES = (4, 2, 4, 2, 4, 4)
-NEAR = ("x", "zl")
-FAR = ("yh", "zh")
+
+def column(x, yh, z):
+    return (x * 2 + yh) * 16 + z
+
+
+def near_groups():
+    order = [(x, z) for x in range(4) for z in NEAR_Z]
+    return [[column(x, yh, zh * 4 + z) for x, z in order] for yh in range(2) for zh in range(4)]
+
+
+def far_groups():
+    order = [(yh, zh) for yh in FAR_Y for zh in FAR_Z]
+    return [[column(x, yh, zh * 4 + z) for yh, zh in order] for x in range(4) for z in range(4)]
+
+
+def line_groups():
+    return [[y * 2 + core for y in LINE_Y] for core in range(2)]
+
+
+NEAR_Z = (2, 1, 0, 3)
+FAR_Y = (1, 0)
+FAR_Z = (2, 3, 1, 0)
+LINE_Y = (1, 2, 0, 3)
+
+
+def exchange(value, axis, groups):
+    return lax.all_to_all(value, axis, 0, 0, axis_index_groups=groups, tiled=True)
 
 
 def split(value):
@@ -150,8 +172,8 @@
     tiles = tiles.reshape(SLOTS, TILE, TILE)
     coords = coords.reshape(2, SLOTS)
     counts = counts.reshape(1)
-    index = lax.axis_index(("x", "yh", "zh", "zl"))
-    core = lax.axis_index("core")
+    index = lax.axis_index("col")
+    core = lax.axis_index("row") % 2
     width = RT * TILE // 128
     spots = (index // 8, index % 8 * width, lane(core), lane(1 - core))
     params = pltpu.CompilerParams(vmem_limit_bytes=8 * MIB)
@@ -178,16 +200,16 @@
             compiler_params=params,
             cost_estimate=pl.CostEstimate(flops=FLOPS, bytes_accessed=1900000, transcendentals=0),
         )(counts, *[pltpu.with_memory_space_constraint(a, pltpu.HBM) for a in (coords, tiles, basis)])
+    part, counts, *spots = lax.optimization_barrier((part, counts) + spots)
+    own_tile, own_column, core_lane, other_lane = spots
     with jax.named_scope("image_near_sum"):
-        got = lax.all_to_all(part, NEAR, 0, 0, tiled=True)
+        got = exchange(part, "col", near_groups())
         near = sum_copies(got, 8)
     with jax.named_scope("image_far_sum"):
-        got = lax.all_to_all(near, FAR, 0, 0, tiled=True)
-        got, counts, *spots = lax.optimization_barrier((got, counts) + spots)
-        own_tile, own_column, core_lane, other_lane = spots
+        got = exchange(near, "col", far_groups())
         row_tile = sum_copies(got, RT)
     with jax.named_scope("image_gather"):
-        image = lax.all_to_all(row_tile, NEAR, 0, 0, tiled=True)
+        image = exchange(row_tile, "col", near_groups())
     with jax.named_scope("image_out"):
         own = lax.dynamic_slice(image, (own_tile, 0, own_column), (1, K, width))[0]
     with jax.named_scope("backward"):
@@ -201,35 +223,32 @@
             compiler_params=params,
             cost_estimate=pl.CostEstimate(flops=FLOPS, bytes_accessed=1900000, transcendentals=0),
         )(places, counts, core_lane, high, low, image)
-    swap = [(0, 1), (1, 0)]
+    swap = [(r, r ^ 1) for r in range(8)]
     with jax.named_scope("back_core_sum"):
-        theirs, own = lax.optimization_barrier((lax.ppermute(send, "core", swap), own))
+        theirs, own = lax.optimization_barrier((lax.ppermute(send, "row", swap), own))
         both = keep + theirs
     with jax.named_scope("back_row_sum"):
-        got = lax.all_to_all(both, "yl", 0, 0, tiled=True)
+        got = exchange(both, "row", line_groups())
         quarter = sum_copies(got.reshape(4, 4 * K, TILE), 4)
     with jax.named_scope("back_row_gather"):
-        mine = lax.all_to_all(quarter.reshape(CT // 2, K, TILE), "yl", 0, 0, tiled=True)
+        mine = exchange(quarter.reshape(CT // 2, K, TILE), "row", line_groups())
     with jax.named_scope("back_core_gather"):
-        other = lax.ppermute(mine, "core", swap)
+        other = lax.ppermute(mine, "row", swap)
         back = place(core_lane, mine)
         back = place(other_lane, other, back)
     return own, back
 
 
 def solution(mesh):
-    fine = Mesh(mesh.devices.reshape(SIZES), AXES)
-    row = ("yl", "core")
-    col = ("x", "yh", "zh", "zl")
     return jax.shard_map(
         per_device,
-        mesh=fine,
+        mesh=mesh,
         in_specs=(
-            P(row, col, None, None, None),
-            P(row, col, None, None),
-            P(row, col),
-            P(None, col),
+            P("row", "col", None, None, None),
+            P("row", "col", None, None),
+            P("row", "col"),
+            P(None, "col"),
         ),
-        out_specs=(P(None, row + col), P(None, col)),
+        out_specs=(P(None, ("row", "col")), P(None, "col")),
         check_vma=False,
     )

time: 111 us -> 95.1 us (0.86)
  blocking collectives: 50.1 us -> 76.5 us
  starting transfers between devices: 36.5 us -> 10.8 us
  waiting for transfers between devices: 17.2 us -> 0.65 us
    all_to_all x4 -> x5, blocking collectives: 50.1 us -> 76.5 us  [exchange(): lax.all_to_all(value, axis, 0, 0, axis_index_groups=groups, tiled=True)]
    all_to_all x1 -> x0, starting transfers between devices: 23.6 us -> none  [per_device(): got = lax.all_to_all(near, FAR, 0, 0, tiled=True)]
    all_to_all x1 -> x0, waiting for transfers between devices: 16.5 us -> none  [per_device(): got = lax.all_to_all(near, FAR, 0, 0, tiled=True)]
    ppermute x2, starting transfers between devices: 12.9 us -> 10.8 us  [the longest x1 5.65 us: per_device(): lax.ppermute(send, 'row', swap)]
  transfers between devices with their start and end apart: 3 -> 2, of which waited for: 3 -> 2; matrix products, arithmetic and copies ran while one was open for 1% -> 1% of each run, Pallas kernels for 1% -> 1%
where the time goes in v3:
time: 95.1 us; the launch traced here: 94.7 us
  blocking collectives  76.5 us (80%)
  starting transfers between devices  10.8 us (11%)
  Pallas kernels  4.55 us (5%)
  between operations  1.4 us (1%)
    all_to_all x5, blocking collectives, exchange(): lax.all_to_all(value, axis, 0, 0, axis_index_groups=groups, tiled=True)  76.5 us
    ppermute x1, starting transfers between devices, per_device(): lax.ppermute(send, 'row', swap)  5.65 us
    ppermute x1, starting transfers between devices, per_device(): other = lax.ppermute(mine, 'row', swap)  5.14 us
    pallas_call x1, Pallas kernels, per_device(): pl.pallas_call(forward_kernel, out_shape=[jax.ShapeDtypeStruct((RT, K, TI...  1.94 us
  transfers between devices with their start and end apart: 2, of which 2 were waited for; matrix products, arithmetic and copies ran while one was open for 1% of the time, Pallas kernels for 1%

profile of v3, /device:TPU:1, one launch (start us, length us, event | category | flops | bytes accessed | tf_op | source)
XLA Modules:
  0.0 94.7 jit_solution(15104307184766146240)
XLA Ops:
  1.3 1.9 %forward.1 = (f32[16,32,128]{2,1,0:T(8,128)S(1)}, bf16[16,128,128]{2,1,0:T(8,128)(2,1)S(1)}, bf16[16,128,128]{2,1,0:T(8,128)(2,1)S(1)}, s32[2,16]{1,0:T(2,128)S(1)}) custom-call(s32[1]{0:T(128)} %bitcast.7.counts, s32[2,16]{1,0:T(2,128)} %bitcast.12, f32[16,128,128]{2,1,0:T(8,128)} %bitcast.10, f32[32,4096]{1,0:T(8,128)} %basis_in.1), custom_call_target="tpu_custom_call" | custom-call | flops 16777216 | bytes 1900000 | tf_op jit(solution)/shard_map/forward/pallas_call | solution.py:182
  3.3 16.4 %all_to_all.25.parts = f32[16,32,128]{2,1,0:T(8,128)S(1)} all-to-all(f32[16,32,128]{2,1,0:T(8,128)S(1)} %get-tuple-element.22), channel_id=1, replica_groups={{2,1,0,3,34,33,32,35,66,65,64,67,98,97,96,99},{6,5,4,7,38,37,36,39,70,6..., dimensions={0} | all-to-all | bytes 524288 | tf_op jit(solution)/shard_map/image_near_sum/all_to_all | solution.py:41
  19.7 28.7 %all_to_all.26.parts = f32[8,32,128]{2,1,0:T(8,128)S(1)} all-to-all(f32[8,32,128]{2,1,0:T(8,128)S(1)} %image_near_sum.1), channel_id=1, replica_groups={{24,28,20,16,8,12,4,0},{25,29,21,17,9,13,5,1},{26,30,22,18,10,14,6,2},{..., dimensions={0} | all-to-all | bytes 262144 | tf_op jit(solution)/shard_map/image_far_sum/all_to_all | solution.py:41
  48.4 14.5 %all_to_all.27.image = f32[16,32,128]{2,1,0:T(8,128)S(1)} all-to-all(f32[16,32,128]{2,1,0:T(8,128)S(1)} %image_far_sum.1), channel_id=1, replica_groups={{2,1,0,3,34,33,32,35,66,65,64,67,98,97,96,99},{6,5,4,7,38,37,36,39,70,6..., dimensions={0} | all-to-all | bytes 524288 | tf_op jit(solution)/shard_map/image_gather/all_to_all | solution.py:41
  62.9 0.8 backward.1
  63.7 5.6 %collective-permute-start = (f32[16,32,128]{2,1,0:T(8,128)S(1)}, f32[16,32,128]{2,1,0:T(8,128)S(1)}, u32[]{:S(2)}, u32[]{:S(2)}) collective-permute-start(f32[16,32,128]{2,1,0:T(8,128)S(1)} %get-tuple-element.23), channel_id=1, source_target_pairs={{0,128},{128,0},{256,384},{384,256},{512,640},{640,512},{768,896},... | collective-permute-start | bytes 786440 | tf_op jit(solution)/shard_map/back_core_sum/ppermute | solution.py:228
  69.4 0.1 constant_dynamic-slice_fusion
  69.5 0.7 copy.7
  70.2 0.4 collective-permute-done
  70.6 8.6 %all_to_all.28 = f32[16,32,128]{2,1,0:T(8,128)S(1)} all-to-all(f32[16,32,128]{2,1,0:T(8,128)S(1)} %add.21), channel_id=1, replica_groups={{256,512,0,768},{384,640,128,896},{257,513,1,769},{385,641,129,897},{25..., dimensions={0} | all-to-all | bytes 524288 | tf_op jit(solution)/shard_map/back_row_sum/all_to_all | solution.py:41
  79.2 8.3 %all_to_all.29.part = f32[16,32,128]{2,1,0:T(8,128)S(1)} all-to-all(f32[16,32,128]{2,1,0:T(8,128)S(1)} %bitcast.9), channel_id=1, replica_groups={{256,512,0,768},{384,640,128,896},{257,513,1,769},{385,641,129,897},{25..., dimensions={0} | all-to-all | bytes 524288 | tf_op jit(solution)/shard_map/back_row_gather/all_to_all | solution.py:41
  87.5 5.1 %collective-permute-start.1 = (f32[16,32,128]{2,1,0:T(8,128)S(1)}, f32[16,32,128]{2,1,0:T(8,128)S(1)}, u32[]{:S(2)}, u32[]{:S(2)}) collective-permute-start(f32[16,32,128]{2,1,0:T(8,128)S(1)} %all_to_all.29.part), channel_id=1, source_target_pairs={{0,128},{128,0},{256,384},{384,256},{512,640},{640,512},{768,896},... | collective-permute-start | bytes 786440 | tf_op jit(solution)/shard_map/back_core_gather/ppermute | solution.py:236
  92.7 0.9 back_core_gather.2.refs_0_
  93.5 0.3 collective-permute-done.1.part
  93.8 0.9 back_core_gather.3
  (6 shorter events, 0.1 us)
Async XLA Ops:
  63.7 6.8 %collective-permute-start = (f32[16,32,128]{2,1,0:T(8,128)S(1)}, f32[16,32,128]{2,1,0:T(8,128)S(1)}, u32[]{:S(2)}, u32[]{:S(2)}) collective-permute-start(f32[16,32,128]{2,1,0:T(8,128)S(1)} %get-tuple-element.23), channel_id=1, source_target_pairs={{0,128},{128,0},{256,384},{384,256},{512,640},{640,512},{768,896},... | collective-permute-start | bytes 786440 | tf_op jit(solution)/shard_map/back_core_sum/ppermute | solution.py:228
  87.5 6.3 %collective-permute-start.1 = (f32[16,32,128]{2,1,0:T(8,128)S(1)}, f32[16,32,128]{2,1,0:T(8,128)S(1)}, u32[]{:S(2)}, u32[]{:S(2)}) collective-permute-start(f32[16,32,128]{2,1,0:T(8,128)S(1)} %all_to_all.29.part), channel_id=1, source_target_pairs={{0,128},{128,0},{256,384},{384,256},{512,640},{640,512},{768,896},... | collective-permute-start | bytes 786440 | tf_op jit(solution)/shard_map/back_core_gather/ppermute | solution.py:236

commit v4 on v3

v4 whole, which is shorter than its diff:
```python
import jax
import jax.numpy as jnp
from jax import lax
from jax.experimental import pallas as pl
from jax.experimental.pallas import tpu as pltpu
from jax.sharding import PartitionSpec as P

K = 32
TILE = 128
RT = 16
CT = 32
SLOTS = 16
BATCH = 4
HALF = CT // 2 * TILE


def device(y, core, x, yh, z):
    return ((y * 2 + core) * 4 + x) * 32 + yh * 16 + z


def near_groups():
    order = [(x, z) for x in NEAR_X for z in NEAR_Z]
    return [
        [device(y, core, x, yh, zh * 4 + z) for x, z in order]
        for y in range(4)
        for core in range(2)
        for yh in range(2)
        for zh in range(4)
    ]


def far_groups():
    order = [(yh, zh) for yh in FAR_Y for zh in FAR_Z]
    return [
        [device(y, core, x, yh, zh * 4 + z) for yh, zh in order]
        for y in range(4)
        for core in range(2)
        for x in range(4)
        for z in range(4)
    ]


def line_groups():
    return [
        [device(y, core, x, yh, z) for y in LINE_Y[yh]]
        for core in range(2)
        for x in range(4)
        for yh in range(2)
        for z in range(16)
    ]


NEAR_X = (2, 1, 3, 0)
NEAR_Z = (2, 1, 0, 3)
FAR_Y = (1, 0)
FAR_Z = (2, 3, 1, 0)
LINE_Y = ((2, 1, 0, 3), (1, 2, 0, 3))


def exchange(value, groups):
    return lax.all_to_all(value, ("row", "col"), 0, 0, axis_index_groups=groups, tiled=True)


def split(value):
    high = value.astype(jnp.bfloat16)
    low = (value - high.astype(jnp.float32)).astype(jnp.bfloat16)
    return high, low


def dot3(left, right_high, right_low, contract):
    high, low = split(left)
    dims = (((1,), (contract,)), ((), ()))
    both = lax.dot_general(
        jnp.concatenate([high, low], axis=0), right_high, dims, preferred_element_type=jnp.float32
    )
    rest = lax.dot_general(high, right_low, dims, preferred_element_type=jnp.float32)
    rows = left.shape[0]
    return both[:rows] + (both[rows:] + rest)


def forward_kernel(
    counts, coords_in, tiles_in, basis_in, part, high, low, coords_out, coords, tiles, basis, small, wide, slots
):
    copies = [
        pltpu.make_async_copy(coords_in, coords, small.at[0]),
        pltpu.make_async_copy(coords_in, coords_out, small.at[1]),
    ]
    copies.append(pltpu.make_async_copy(basis_in, basis, wide.at[0]))
    for t in range(SLOTS // BATCH):
        some = pl.ds(t * BATCH, BATCH)
        copies.append(pltpu.make_async_copy(tiles_in.at[some], tiles.at[some], slots.at[t]))
    for copy in copies:
        copy.start()
    part[...] = jnp.zeros_like(part)
    for copy in copies:
        copy.wait()
    live = counts[0]
    for s in range(SLOTS):
        high[s], low[s] = split(tiles[s])
    for s in range(SLOTS):
        row = coords[0, s]
        col = pl.multiple_of(coords[1, s] * TILE, TILE)
        product = dot3(basis[:, pl.ds(col, TILE)], high[s], low[s], 1)
        part[row] += jnp.where(s < live, product, 0.0)


def backward_kernel(coords, counts, core, high, low, image, keep, send, acc):
    acc[...] = jnp.zeros_like(acc)
    live = counts[0]
    for s in range(SLOTS):
        product = dot3(image[coords[0, s]], high[s], low[s], 0)
        col = pl.multiple_of(coords[1, s] * TILE, TILE)
        acc[:, pl.ds(col, TILE)] += jnp.where(s < live, product, 0.0)
    mine = pl.multiple_of(core[0, 0] * HALF, TILE)
    other = pl.multiple_of(HALF - core[0, 0] * HALF, TILE)
    keep[...] = acc[:, pl.ds(mine, HALF)]
    send[...] = acc[:, pl.ds(other, HALF)]


def sum_copies_kernel(parts, copies):
    total = parts[0]
    for p in range(1, parts.shape[0]):
        total = total + parts[p]
    for p in range(copies.shape[0]):
        copies[p] = total


def place_kernel(half, part, *refs):
    back, sem = refs[-2:]
    column = pl.multiple_of(half[0, 0] * HALF, TILE)
    copy = pltpu.make_async_copy(part, back.at[:, pl.ds(column, HALF)], sem.at[0])
    copy.start()
    copy.wait()


SMEM = pl.BlockSpec(memory_space=pltpu.SMEM)
VMEM = pl.BlockSpec(memory_space=pltpu.VMEM)
ANY = pl.BlockSpec(memory_space=pl.ANY)
MIB = 1024 * 1024
FLOPS = 2 * SLOTS * K * TILE * TILE


def sum_copies(parts, copies):
    return pl.pallas_call(
        sum_copies_kernel,
        out_shape=pltpu.VMEM((copies,) + parts.shape[1:], jnp.float32),
        in_specs=[VMEM],
        out_specs=VMEM,
        compiler_params=pltpu.CompilerParams(vmem_limit_bytes=2 * MIB),
        cost_estimate=pl.CostEstimate(
            flops=parts.size, bytes_accessed=4 * (parts.size + copies * parts[0].size), transcendentals=0
        ),
    )(parts)


def lane(value):
    return jnp.broadcast_to(value, (8, TILE))


def place(half, part, *back):
    return pl.pallas_call(
        place_kernel,
        out_shape=jax.ShapeDtypeStruct((K, CT * TILE), jnp.float32),
        in_specs=[VMEM, ANY] + [ANY] * len(back),
        out_specs=ANY,
        scratch_shapes=[pltpu.SemaphoreType.DMA((1,))],
        input_output_aliases={2: 0} if back else {},
        compiler_params=pltpu.CompilerParams(vmem_limit_bytes=2 * MIB),
        cost_estimate=pl.CostEstimate(flops=0, bytes_accessed=600000, transcendentals=0),
    )(half, part, *back)


def per_device(tiles, coords, counts, basis):
    tiles = tiles.reshape(SLOTS, TILE, TILE)
    coords = coords.reshape(2, SLOTS)
    counts = counts.reshape(1)
    index = lax.axis_index("col")
    core = lax.axis_index("row") % 2
    width = RT * TILE // 128
    spots = (index // 8, index % 8 * width, lane(core), lane(1 - core))
    params = pltpu.CompilerParams(vmem_limit_bytes=8 * MIB)
    halves = jax.ShapeDtypeStruct((SLOTS, TILE, TILE), jnp.bfloat16)
    with jax.named_scope("forward"):
        part, high, low, places = pl.pallas_call(
            forward_kernel,
            out_shape=[
                jax.ShapeDtypeStruct((RT, K, TILE), jnp.float32),
                halves,
                halves,
                jax.ShapeDtypeStruct((2, SLOTS), jnp.int32),
            ],
            in_specs=[SMEM] + [ANY] * 3,
            out_specs=[VMEM] * 4,
            scratch_shapes=[
                pltpu.SMEM((2, SLOTS), jnp.int32),
                pltpu.VMEM((SLOTS, TILE, TILE), jnp.float32),
                pltpu.VMEM((K, CT * TILE), jnp.float32),
                pltpu.SemaphoreType.DMA((2,)),
                pltpu.SemaphoreType.DMA((1,)),
                pltpu.SemaphoreType.DMA((SLOTS // BATCH,)),
            ],
            compiler_params=params,
            cost_estimate=pl.CostEstimate(flops=FLOPS, bytes_accessed=1900000, transcendentals=0),
        )(counts, *[pltpu.with_memory_space_constraint(a, pltpu.HBM) for a in (coords, tiles, basis)])
    part, counts, *spots = lax.optimization_barrier((part, counts) + spots)
    own_tile, own_column, core_lane, other_lane = spots
    with jax.named_scope("image_near_sum"):
        got = exchange(part, near_groups())
        near = sum_copies(got, 8)
    with jax.named_scope("image_far_sum"):
        got = exchange(near, far_groups())
        row_tile = sum_copies(got, RT)
    with jax.named_scope("image_gather"):
        image = exchange(row_tile, near_groups())
    with jax.named_scope("image_out"):
        own = lax.dynamic_slice(image, (own_tile, 0, own_column), (1, K, width))[0]
    with jax.named_scope("backward"):
        half = jax.ShapeDtypeStruct((K, HALF), jnp.float32)
        keep, send = pl.pallas_call(
            backward_kernel,
            out_shape=[half, half],
            in_specs=[SMEM, SMEM, VMEM, VMEM, VMEM, VMEM],
            out_specs=[VMEM, VMEM],
            scratch_shapes=[pltpu.VMEM((K, CT * TILE), jnp.float32)],
            compiler_params=params,
            cost_estimate=pl.CostEstimate(flops=FLOPS, bytes_accessed=1900000, transcendentals=0),
        )(places, counts, core_lane, high, low, image)
    swap = [(r, r ^ 1) for r in range(8)]
    with jax.named_scope("back_core_sum"):
        theirs, own = lax.optimization_barrier((lax.ppermute(send, "row", swap), own))
        both = keep + theirs
    with jax.named_scope("back_row_sum"):
        got = exchange(both, line_groups())
        quarter = sum_copies(got.reshape(4, K // 4, HALF), 4)
    with jax.named_scope("back_row_gather"):
        mine = exchange(quarter.reshape(K, HALF), line_groups())
    with jax.named_scope("back_core_gather"):
        other = lax.ppermute(mine, "row", swap)
        back = place(core_lane, mine)
        back = place(other_lane, other, back)
    return own, back


def solution(mesh):
    return jax.shard_map(
        per_device,
        mesh=mesh,
        in_specs=(
            P("row", "col", None, None, None),
            P("row", "col", None, None),
            P("row", "col"),
            P(None, "col"),
        ),
        out_specs=(P(None, ("row", "col")), P(None, "col")),
        check_vma=False,
    )
```

time: 95.1 us -> 93.1 us (0.979)
  blocking collectives: 76.5 us -> 73.4 us
    all_to_all x5, blocking collectives: 76.5 us -> 73.4 us  [exchange(): lax.all_to_all(value, ('row', 'col'), 0, 0, axis_index_groups=groups, til...]
where the time goes in v4:
time: 93.1 us; the launch traced here: 92.8 us
  blocking collectives  73.4 us (79%)
  starting transfers between devices  11.7 us (13%)
  Pallas kernels  4.75 us (5%)
  between operations  1.39 us (1%)
    all_to_all x5, blocking collectives, exchange(): lax.all_to_all(value, ('row', 'col'), 0, 0, axis_index_groups=groups, til...  73.4 us
    ppermute x1, starting transfers between devices, per_device(): lax.ppermute(send, 'row', swap)  6.6 us
    ppermute x1, starting transfers between devices, per_device(): other = lax.ppermute(mine, 'row', swap)  5.08 us
    pallas_call x1, Pallas kernels, per_device(): pl.pallas_call(forward_kernel, out_shape=[jax.ShapeDtypeStruct((RT, K, TI...  2.19 us
  transfers between devices with their start and end apart: 2, of which 2 were waited for; matrix products, arithmetic and copies ran while one was open for 1% of the time, Pallas kernels for 1%

profile of v4, /device:TPU:1, one launch (start us, length us, event | category | flops | bytes accessed | tf_op | source)
XLA Modules:
  0.0 92.8 jit_solution(14307808303362736702)
XLA Ops:
  1.3 2.2 %forward.1 = (f32[16,32,128]{2,1,0:T(8,128)S(1)}, bf16[16,128,128]{2,1,0:T(8,128)(2,1)S(1)}, bf16[16,128,128]{2,1,0:T(8,128)(2,1)S(1)}, s32[2,16]{1,0:T(2,128)S(1)}) custom-call(s32[1]{0:T(128)} %bitcast.8.counts, s32[2,16]{1,0:T(2,128)} %bitcast.13, f32[16,128,128]{2,1,0:T(8,128)} %bitcast.11, f32[32,4096]{1,0:T(8,128)} %basis_in.1), custom_call_target="tpu_custom_call" | custom-call | flops 16777216 | bytes 1900000 | tf_op jit(solution)/shard_map/forward/pallas_call | solution.py:184
  3.5 15.3 %all_to_all.32.parts = f32[16,32,128]{2,1,0:T(8,128)S(1)} all-to-all(f32[16,32,128]{2,1,0:T(8,128)S(1)} %get-tuple-element.22), channel_id=1, replica_groups={{66,65,64,67,34,33,32,35,98,97,96,99,2,1,0,3},{70,69,68,71,38,37,36,39,..., dimensions={0} | all-to-all | bytes 524288 | tf_op jit(solution)/shard_map/image_near_sum/all_to_all | solution.py:61
  18.8 28.3 %all_to_all.33.parts = f32[8,32,128]{2,1,0:T(8,128)S(1)} all-to-all(f32[8,32,128]{2,1,0:T(8,128)S(1)} %image_near_sum.1), channel_id=1, replica_groups={{24,28,20,16,8,12,4,0},{25,29,21,17,9,13,5,1},{26,30,22,18,10,14,6,2},{..., dimensions={0} | all-to-all | bytes 262144 | tf_op jit(solution)/shard_map/image_far_sum/all_to_all | solution.py:61
  47.2 12.0 %all_to_all.34.image = f32[16,32,128]{2,1,0:T(8,128)S(1)} all-to-all(f32[16,32,128]{2,1,0:T(8,128)S(1)} %image_far_sum.1), channel_id=1, replica_groups={{66,65,64,67,34,33,32,35,98,97,96,99,2,1,0,3},{70,69,68,71,38,37,36,39,..., dimensions={0} | all-to-all | bytes 524288 | tf_op jit(solution)/shard_map/image_gather/all_to_all | solution.py:61
  59.2 1.0 %backward.1 = (f32[32,2048]{1,0:T(8,128)S(1)}, f32[32,2048]{1,0:T(8,128)S(1)}) custom-call(s32[2,16]{1,0:T(2,128)S(1)} %get-tuple-element.16.coords, s32[1]{0:T(128)} %bitcast.7.counts, s32[8,128]{1,0:T(8,128)S(1)} %broadcast_in_dim.6.core.half, bf16[16,128,128]{2,1,0:T(8,128)(2,1)S(1)} %get-tuple-element.20.high, ...), custom_call_target="tpu_custom_call" | custom-call | flops 16777216 | bytes 1900000 | tf_op jit(solution)/shard_map/backward/pallas_call | solution.py:219
  60.2 6.6 %collective-permute-start = (f32[32,2048]{1,0:T(8,128)S(1)}, f32[32,2048]{1,0:T(8,128)S(1)}, u32[]{:S(2)}, u32[]{:S(2)}) collective-permute-start(f32[32,2048]{1,0:T(8,128)S(1)} %get-tuple-element.23), channel_id=1, source_target_pairs={{0,128},{128,0},{256,384},{384,256},{512,640},{640,512},{768,896},... | collective-permute-start | bytes 786440 | tf_op jit(solution)/shard_map/back_core_sum/ppermute | solution.py:230
  66.8 0.1 constant_dynamic-slice_fusion
  66.9 0.7 copy.7
  67.6 0.4 collective-permute-done
  68.0 9.3 %all_to_all.35.parts = f32[4,8,2048]{2,1,0:T(8,128)S(1)} all-to-all(f32[4,8,2048]{2,1,0:T(8,128)S(1)} %add_bitcast_fusion), channel_id=1, replica_groups={{512,256,0,768},{513,257,1,769},{514,258,2,770},{515,259,3,771},{516,26..., dimensions={0} | all-to-all | bytes 524288 | tf_op jit(solution)/shard_map/back_row_sum/all_to_all | solution.py:61
  77.3 8.5 %all_to_all.36 = f32[4,8,2048]{2,1,0:T(8,128)S(1)} all-to-all(f32[4,8,2048]{2,1,0:T(8,128)S(1)} %back_row_sum.1), channel_id=1, replica_groups={{512,256,0,768},{513,257,1,769},{514,258,2,770},{515,259,3,771},{516,26..., dimensions={0} | all-to-all | bytes 524288 | tf_op jit(solution)/shard_map/back_row_gather/all_to_all | solution.py:61
  85.8 5.1 %collective-permute-start.1 = (f32[32,2048]{1,0:T(8,128)S(1)}, f32[32,2048]{1,0:T(8,128)S(1)}, u32[]{:S(2)}, u32[]{:S(2)}) collective-permute-start(f32[32,2048]{1,0:T(8,128)S(1)} %bitcast.9), channel_id=1, source_target_pairs={{0,128},{128,0},{256,384},{384,256},{512,640},{640,512},{768,896},... | collective-permute-start | bytes 786440 | tf_op jit(solution)/shard_map/back_core_gather/ppermute | solution.py:238
  90.9 0.7 back_core_gather.2.refs_0_
  91.6 0.4 collective-permute-done.1.part
  92.0 0.7 back_core_gather.3
  (6 shorter events, 0.1 us)
Async XLA Ops:
  60.2 7.7 %collective-permute-start = (f32[32,2048]{1,0:T(8,128)S(1)}, f32[32,2048]{1,0:T(8,128)S(1)}, u32[]{:S(2)}, u32[]{:S(2)}) collective-permute-start(f32[32,2048]{1,0:T(8,128)S(1)} %get-tuple-element.23), channel_id=1, source_target_pairs={{0,128},{128,0},{256,384},{384,256},{512,640},{640,512},{768,896},... | collective-permute-start | bytes 786440 | tf_op jit(solution)/shard_map/back_core_sum/ppermute | solution.py:230
  85.8 6.2 %collective-permute-start.1 = (f32[32,2048]{1,0:T(8,128)S(1)}, f32[32,2048]{1,0:T(8,128)S(1)}, u32[]{:S(2)}, u32[]{:S(2)}) collective-permute-start(f32[32,2048]{1,0:T(8,128)S(1)} %bitcast.9), channel_id=1, source_target_pairs={{0,128},{128,0},{256,384},{384,256},{512,640},{640,512},{768,896},... | collective-permute-start | bytes 786440 | tf_op jit(solution)/shard_map/back_core_gather/ppermute | solution.py:238

commit v5 on v4

--- a/solution.py
+++ b/solution.py
@@ -79,11 +79,12 @@
 
 
 def forward_kernel(
-    counts, coords_in, tiles_in, basis_in, part, high, low, coords_out, coords, tiles, basis, small, wide, slots
+    counts_in, coords_in, tiles_in, basis_in, part, high, low, places, counts, coords, tiles, basis, small, wide, slots
 ):
     copies = [
         pltpu.make_async_copy(coords_in, coords, small.at[0]),
-        pltpu.make_async_copy(coords_in, coords_out, small.at[1]),
+        pltpu.make_async_copy(coords_in, places, small.at[1]),
+        pltpu.make_async_copy(counts_in, counts, small.at[2]),
     ]
     copies.append(pltpu.make_async_copy(basis_in, basis, wide.at[0]))
     for t in range(SLOTS // BATCH):
@@ -95,6 +96,8 @@
     for copy in copies:
         copy.wait()
     live = counts[0]
+    slot = lax.broadcasted_iota(jnp.int32, places.shape, 1)
+    places[...] = jnp.where(slot < live, places[...], -1)
     for s in range(SLOTS):
         high[s], low[s] = split(tiles[s])
     for s in range(SLOTS):
@@ -104,13 +107,13 @@
         part[row] += jnp.where(s < live, product, 0.0)
 
 
-def backward_kernel(coords, counts, core, high, low, image, keep, send, acc):
+def backward_kernel(places, core, high, low, image, keep, send, acc):
     acc[...] = jnp.zeros_like(acc)
-    live = counts[0]
     for s in range(SLOTS):
-        product = dot3(image[coords[0, s]], high[s], low[s], 0)
-        col = pl.multiple_of(coords[1, s] * TILE, TILE)
-        acc[:, pl.ds(col, TILE)] += jnp.where(s < live, product, 0.0)
+        row = places[0, s]
+        product = dot3(image[jnp.maximum(row, 0)], high[s], low[s], 0)
+        col = pl.multiple_of(jnp.maximum(places[1, s], 0) * TILE, TILE)
+        acc[:, pl.ds(col, TILE)] += jnp.where(row >= 0, product, 0.0)
     mine = pl.multiple_of(core[0, 0] * HALF, TILE)
     other = pl.multiple_of(HALF - core[0, 0] * HALF, TILE)
     keep[...] = acc[:, pl.ds(mine, HALF)]
@@ -189,20 +192,21 @@
                 halves,
                 jax.ShapeDtypeStruct((2, SLOTS), jnp.int32),
             ],
-            in_specs=[SMEM] + [ANY] * 3,
+            in_specs=[ANY] * 4,
             out_specs=[VMEM] * 4,
             scratch_shapes=[
+                pltpu.SMEM((1,), jnp.int32),
                 pltpu.SMEM((2, SLOTS), jnp.int32),
                 pltpu.VMEM((SLOTS, TILE, TILE), jnp.float32),
                 pltpu.VMEM((K, CT * TILE), jnp.float32),
-                pltpu.SemaphoreType.DMA((2,)),
+                pltpu.SemaphoreType.DMA((3,)),
                 pltpu.SemaphoreType.DMA((1,)),
                 pltpu.SemaphoreType.DMA((SLOTS // BATCH,)),
             ],
             compiler_params=params,
             cost_estimate=pl.CostEstimate(flops=FLOPS, bytes_accessed=1900000, transcendentals=0),
         )(counts, *[pltpu.with_memory_space_constraint(a, pltpu.HBM) for a in (coords, tiles, basis)])
-    part, counts, *spots = lax.optimization_barrier((part, counts) + spots)
+    part, *spots = lax.optimization_barrier((part,) + spots)
     own_tile, own_column, core_lane, other_lane = spots
     with jax.named_scope("image_near_sum"):
         got = exchange(part, near_groups())
@@ -219,12 +223,12 @@
         keep, send = pl.pallas_call(
             backward_kernel,
             out_shape=[half, half],
-            in_specs=[SMEM, SMEM, VMEM, VMEM, VMEM, VMEM],
+            in_specs=[VMEM, VMEM, VMEM, VMEM, VMEM],
             out_specs=[VMEM, VMEM],
             scratch_shapes=[pltpu.VMEM((K, CT * TILE), jnp.float32)],
             compiler_params=params,
             cost_estimate=pl.CostEstimate(flops=FLOPS, bytes_accessed=1900000, transcendentals=0),
-        )(places, counts, core_lane, high, low, image)
+        )(places, core_lane, high, low, image)
     swap = [(r, r ^ 1) for r in range(8)]
     with jax.named_scope("back_core_sum"):
         theirs, own = lax.optimization_barrier((lax.ppermute(send, "row", swap), own))

time: 93.1 us -> 92.7 us (level)
  no operation moved by 1% of the time
where the time goes in v5:
time: 92.7 us; the launch traced here: 92.3 us
  blocking collectives  73.4 us (79%)
  starting transfers between devices  11.7 us (13%)
  Pallas kernels  4.31 us (5%)
  between operations  1.4 us (2%)
    all_to_all x5, blocking collectives, exchange(): lax.all_to_all(value, ('row', 'col'), 0, 0, axis_index_groups=groups, til...  73.4 us
    ppermute x1, starting transfers between devices, per_device(): lax.ppermute(send, 'row', swap)  6.59 us
    ppermute x1, starting transfers between devices, per_device(): other = lax.ppermute(mine, 'row', swap)  5.09 us
    pallas_call x1, Pallas kernels, per_device(): pl.pallas_call(forward_kernel, out_shape=[jax.ShapeDtypeStruct((RT, K, TI...  2.2 us
  transfers between devices with their start and end apart: 2, of which 2 were waited for; matrix products, arithmetic and copies ran while one was open for 1% of the time, Pallas kernels for 1%

profile of v5, /device:TPU:1, one launch (start us, length us, event | category | flops | bytes accessed | tf_op | source)
XLA Modules:
  0.0 92.3 jit_solution(3983233838411719907)
XLA Ops:
  1.3 2.2 %forward.1 = (f32[16,32,128]{2,1,0:T(8,128)S(1)}, bf16[16,128,128]{2,1,0:T(8,128)(2,1)S(1)}, bf16[16,128,128]{2,1,0:T(8,128)(2,1)S(1)}, s32[2,16]{1,0:T(2,128)S(1)}) custom-call(s32[1]{0:T(128)} %bitcast.7.counts_in, s32[2,16]{1,0:T(2,128)} %bitcast.12, f32[16,128,128]{2,1,0:T(8,128)} %bitcast.10, f32[32,4096]{1,0:T(8,128)} %basis_in.1), custom_call_target="tpu_custom_call" | custom-call | flops 16777216 | bytes 1900000 | tf_op jit(solution)/shard_map/forward/pallas_call | solution.py:187
  3.5 15.3 %all_to_all.32.parts = f32[16,32,128]{2,1,0:T(8,128)S(1)} all-to-all(f32[16,32,128]{2,1,0:T(8,128)S(1)} %get-tuple-element.20), channel_id=1, replica_groups={{66,65,64,67,34,33,32,35,98,97,96,99,2,1,0,3},{70,69,68,71,38,37,36,39,..., dimensions={0} | all-to-all | bytes 524288 | tf_op jit(solution)/shard_map/image_near_sum/all_to_all | solution.py:61
  18.8 28.3 %all_to_all.33.parts = f32[8,32,128]{2,1,0:T(8,128)S(1)} all-to-all(f32[8,32,128]{2,1,0:T(8,128)S(1)} %image_near_sum.1), channel_id=1, replica_groups={{24,28,20,16,8,12,4,0},{25,29,21,17,9,13,5,1},{26,30,22,18,10,14,6,2},{..., dimensions={0} | all-to-all | bytes 262144 | tf_op jit(solution)/shard_map/image_far_sum/all_to_all | solution.py:61
  47.2 12.0 %all_to_all.34.image = f32[16,32,128]{2,1,0:T(8,128)S(1)} all-to-all(f32[16,32,128]{2,1,0:T(8,128)S(1)} %image_far_sum.1), channel_id=1, replica_groups={{66,65,64,67,34,33,32,35,98,97,96,99,2,1,0,3},{70,69,68,71,38,37,36,39,..., dimensions={0} | all-to-all | bytes 524288 | tf_op jit(solution)/shard_map/image_gather/all_to_all | solution.py:61
  59.2 0.5 backward.1
  59.8 6.6 %collective-permute-start = (f32[32,2048]{1,0:T(8,128)S(1)}, f32[32,2048]{1,0:T(8,128)S(1)}, u32[]{:S(2)}, u32[]{:S(2)}) collective-permute-start(f32[32,2048]{1,0:T(8,128)S(1)} %get-tuple-element.21), channel_id=1, source_target_pairs={{0,128},{128,0},{256,384},{384,256},{512,640},{640,512},{768,896},... | collective-permute-start | bytes 786440 | tf_op jit(solution)/shard_map/back_core_sum/ppermute | solution.py:234
  66.4 0.1 constant_dynamic-slice_fusion
  66.5 0.7 copy.7
  67.2 0.4 collective-permute-done
  67.6 9.3 %all_to_all.35.parts = f32[4,8,2048]{2,1,0:T(8,128)S(1)} all-to-all(f32[4,8,2048]{2,1,0:T(8,128)S(1)} %add_bitcast_fusion), channel_id=1, replica_groups={{512,256,0,768},{513,257,1,769},{514,258,2,770},{515,259,3,771},{516,26..., dimensions={0} | all-to-all | bytes 524288 | tf_op jit(solution)/shard_map/back_row_sum/all_to_all | solution.py:61
  76.9 8.5 %all_to_all.36 = f32[4,8,2048]{2,1,0:T(8,128)S(1)} all-to-all(f32[4,8,2048]{2,1,0:T(8,128)S(1)} %back_row_sum.1), channel_id=1, replica_groups={{512,256,0,768},{513,257,1,769},{514,258,2,770},{515,259,3,771},{516,26..., dimensions={0} | all-to-all | bytes 524288 | tf_op jit(solution)/shard_map/back_row_gather/all_to_all | solution.py:61
  85.3 5.1 %collective-permute-start.1 = (f32[32,2048]{1,0:T(8,128)S(1)}, f32[32,2048]{1,0:T(8,128)S(1)}, u32[]{:S(2)}, u32[]{:S(2)}) collective-permute-start(f32[32,2048]{1,0:T(8,128)S(1)} %bitcast.8), channel_id=1, source_target_pairs={{0,128},{128,0},{256,384},{384,256},{512,640},{640,512},{768,896},... | collective-permute-start | bytes 786440 | tf_op jit(solution)/shard_map/back_core_gather/ppermute | solution.py:242
  90.4 0.7 back_core_gather.2.refs_0_
  91.2 0.4 collective-permute-done.1.part
  91.6 0.7 back_core_gather.3
  (6 shorter events, 0.1 us)
Async XLA Ops:
  59.8 7.7 %collective-permute-start = (f32[32,2048]{1,0:T(8,128)S(1)}, f32[32,2048]{1,0:T(8,128)S(1)}, u32[]{:S(2)}, u32[]{:S(2)}) collective-permute-start(f32[32,2048]{1,0:T(8,128)S(1)} %get-tuple-element.21), channel_id=1, source_target_pairs={{0,128},{128,0},{256,384},{384,256},{512,640},{640,512},{768,896},... | collective-permute-start | bytes 786440 | tf_op jit(solution)/shard_map/back_core_sum/ppermute | solution.py:234
  85.3 6.2 %collective-permute-start.1 = (f32[32,2048]{1,0:T(8,128)S(1)}, f32[32,2048]{1,0:T(8,128)S(1)}, u32[]{:S(2)}, u32[]{:S(2)}) collective-permute-start(f32[32,2048]{1,0:T(8,128)S(1)} %bitcast.8), channel_id=1, source_target_pairs={{0,128},{128,0},{256,384},{384,256},{512,640},{640,512},{768,896},... | collective-permute-start | bytes 786440 | tf_op jit(solution)/shard_map/back_core_gather/ppermute | solution.py:242

commit v6 on v5

--- a/solution.py
+++ b/solution.py
@@ -10,7 +10,7 @@
 RT = 16
 CT = 32
 SLOTS = 16
-BATCH = 4
+BATCH = 8
 HALF = CT // 2 * TILE
 
 
@@ -19,7 +19,7 @@
 
 
 def near_groups():
-    order = [(x, z) for x in NEAR_X for z in NEAR_Z]
+    order = [NEAR_FIRST] + [(x, z) for z in range(4) for x in range(4) if (x, z) != NEAR_FIRST]
     return [
         [device(y, core, x, yh, zh * 4 + z) for x, z in order]
         for y in range(4)
@@ -30,7 +30,7 @@
 
 
 def far_groups():
-    order = [(yh, zh) for yh in FAR_Y for zh in FAR_Z]
+    order = [FAR_FIRST] + [(yh, zh) for zh in range(4) for yh in range(2) if (yh, zh) != FAR_FIRST]
     return [
         [device(y, core, x, yh, zh * 4 + z) for yh, zh in order]
         for y in range(4)
@@ -50,10 +50,8 @@
     ]
 
 
-NEAR_X = (2, 1, 3, 0)
-NEAR_Z = (2, 1, 0, 3)
-FAR_Y = (1, 0)
-FAR_Z = (2, 3, 1, 0)
+NEAR_FIRST = (2, 2)
+FAR_FIRST = (1, 2)
 LINE_Y = ((2, 1, 0, 3), (1, 2, 0, 3))
 
 

time: 92.7 us -> 93.2 us (level)
  no operation moved by 1% of the time
where the time goes in v6:
time: 93.2 us; the launch traced here: 92.8 us
  blocking collectives  73.3 us (79%)
  starting transfers between devices  12.2 us (13%)
  Pallas kernels  4.3 us (5%)
  between operations  1.4 us (2%)
    all_to_all x5, blocking collectives, exchange(): lax.all_to_all(value, ('row', 'col'), 0, 0, axis_index_groups=groups, til...  73.3 us
    ppermute x1, starting transfers between devices, per_device(): lax.ppermute(send, 'row', swap)  7.1 us
    ppermute x1, starting transfers between devices, per_device(): other = lax.ppermute(mine, 'row', swap)  5.08 us
    pallas_call x1, Pallas kernels, per_device(): pl.pallas_call(forward_kernel, out_shape=[jax.ShapeDtypeStruct((RT, K, TI...  2.2 us
  transfers between devices with their start and end apart: 2, of which 2 were waited for; matrix products, arithmetic and copies ran while one was open for 1% of the time, Pallas kernels for 1%

profile of v6, /device:TPU:1, one launch (start us, length us, event | category | flops | bytes accessed | tf_op | source)
XLA Modules:
  0.0 92.8 jit_solution(4193258480546494280)
XLA Ops:
  1.3 2.2 %forward.1 = (f32[16,32,128]{2,1,0:T(8,128)S(1)}, bf16[16,128,128]{2,1,0:T(8,128)(2,1)S(1)}, bf16[16,128,128]{2,1,0:T(8,128)(2,1)S(1)}, s32[2,16]{1,0:T(2,128)S(1)}) custom-call(s32[1]{0:T(128)} %bitcast.7.counts_in, s32[2,16]{1,0:T(2,128)} %bitcast.12, f32[16,128,128]{2,1,0:T(8,128)} %bitcast.10, f32[32,4096]{1,0:T(8,128)} %basis_in.1), custom_call_target="tpu_custom_call" | custom-call | flops 16777216 | bytes 1900000 | tf_op jit(solution)/shard_map/forward/pallas_call | solution.py:185
  3.5 15.4 %all_to_all.32.parts = f32[16,32,128]{2,1,0:T(8,128)S(1)} all-to-all(f32[16,32,128]{2,1,0:T(8,128)S(1)} %get-tuple-element.20), channel_id=1, replica_groups={{66,0,32,64,96,1,33,65,97,2,34,98,3,35,67,99},{70,4,36,68,100,5,37,69,1..., dimensions={0} | all-to-all | bytes 524288 | tf_op jit(solution)/shard_map/image_near_sum/all_to_all | solution.py:59
  19.0 29.5 %all_to_all.33.parts = f32[8,32,128]{2,1,0:T(8,128)S(1)} all-to-all(f32[8,32,128]{2,1,0:T(8,128)S(1)} %image_near_sum.1), channel_id=1, replica_groups={{24,0,16,4,20,8,12,28},{25,1,17,5,21,9,13,29},{26,2,18,6,22,10,14,30},{..., dimensions={0} | all-to-all | bytes 262144 | tf_op jit(solution)/shard_map/image_far_sum/all_to_all | solution.py:59
  48.5 10.7 %all_to_all.34.image = f32[16,32,128]{2,1,0:T(8,128)S(1)} all-to-all(f32[16,32,128]{2,1,0:T(8,128)S(1)} %image_far_sum.1), channel_id=1, replica_groups={{66,0,32,64,96,1,33,65,97,2,34,98,3,35,67,99},{70,4,36,68,100,5,37,69,1..., dimensions={0} | all-to-all | bytes 524288 | tf_op jit(solution)/shard_map/image_gather/all_to_all | solution.py:59
  59.2 0.5 backward.1
  59.7 7.1 %collective-permute-start = (f32[32,2048]{1,0:T(8,128)S(1)}, f32[32,2048]{1,0:T(8,128)S(1)}, u32[]{:S(2)}, u32[]{:S(2)}) collective-permute-start(f32[32,2048]{1,0:T(8,128)S(1)} %get-tuple-element.21), channel_id=1, source_target_pairs={{0,128},{128,0},{256,384},{384,256},{512,640},{640,512},{768,896},... | collective-permute-start | bytes 786440 | tf_op jit(solution)/shard_map/back_core_sum/ppermute | solution.py:232
  66.9 0.1 constant_dynamic-slice_fusion
  66.9 0.7 copy.7
  67.6 0.4 collective-permute-done
  68.0 9.3 %all_to_all.35.parts = f32[4,8,2048]{2,1,0:T(8,128)S(1)} all-to-all(f32[4,8,2048]{2,1,0:T(8,128)S(1)} %add_bitcast_fusion), channel_id=1, replica_groups={{512,256,0,768},{513,257,1,769},{514,258,2,770},{515,259,3,771},{516,26..., dimensions={0} | all-to-all | bytes 524288 | tf_op jit(solution)/shard_map/back_row_sum/all_to_all | solution.py:59
  77.3 8.5 %all_to_all.36 = f32[4,8,2048]{2,1,0:T(8,128)S(1)} all-to-all(f32[4,8,2048]{2,1,0:T(8,128)S(1)} %back_row_sum.1), channel_id=1, replica_groups={{512,256,0,768},{513,257,1,769},{514,258,2,770},{515,259,3,771},{516,26..., dimensions={0} | all-to-all | bytes 524288 | tf_op jit(solution)/shard_map/back_row_gather/all_to_all | solution.py:59
  85.8 5.1 %collective-permute-start.1 = (f32[32,2048]{1,0:T(8,128)S(1)}, f32[32,2048]{1,0:T(8,128)S(1)}, u32[]{:S(2)}, u32[]{:S(2)}) collective-permute-start(f32[32,2048]{1,0:T(8,128)S(1)} %bitcast.8), channel_id=1, source_target_pairs={{0,128},{128,0},{256,384},{384,256},{512,640},{640,512},{768,896},... | collective-permute-start | bytes 786440 | tf_op jit(solution)/shard_map/back_core_gather/ppermute | solution.py:240
  90.9 0.7 back_core_gather.2.refs_0_
  91.7 0.4 collective-permute-done.1.part
  92.0 0.7 back_core_gather.3
  (6 shorter events, 0.1 us)
Async XLA Ops:
  59.7 8.2 %collective-permute-start = (f32[32,2048]{1,0:T(8,128)S(1)}, f32[32,2048]{1,0:T(8,128)S(1)}, u32[]{:S(2)}, u32[]{:S(2)}) collective-permute-start(f32[32,2048]{1,0:T(8,128)S(1)} %get-tuple-element.21), channel_id=1, source_target_pairs={{0,128},{128,0},{256,384},{384,256},{512,640},{640,512},{768,896},... | collective-permute-start | bytes 786440 | tf_op jit(solution)/shard_map/back_core_sum/ppermute | solution.py:232
  85.8 6.2 %collective-permute-start.1 = (f32[32,2048]{1,0:T(8,128)S(1)}, f32[32,2048]{1,0:T(8,128)S(1)}, u32[]{:S(2)}, u32[]{:S(2)}) collective-permute-start(f32[32,2048]{1,0:T(8,128)S(1)} %bitcast.8), channel_id=1, source_target_pairs={{0,128},{128,0},{256,384},{384,256},{512,640},{640,512},{768,896},... | collective-permute-start | bytes 786440 | tf_op jit(solution)/shard_map/back_core_gather/ppermute | solution.py:240

commit v7 on v5

--- a/solution.py
+++ b/solution.py
@@ -86,20 +86,21 @@
         pltpu.make_async_copy(coords_in, places, small.at[1]),
         pltpu.make_async_copy(counts_in, counts, small.at[2]),
     ]
-    copies.append(pltpu.make_async_copy(basis_in, basis, wide.at[0]))
     for t in range(SLOTS // BATCH):
         some = pl.ds(t * BATCH, BATCH)
         copies.append(pltpu.make_async_copy(tiles_in.at[some], tiles.at[some], slots.at[t]))
+    copies.append(pltpu.make_async_copy(basis_in, basis, wide.at[0]))
     for copy in copies:
         copy.start()
     part[...] = jnp.zeros_like(part)
-    for copy in copies:
+    for copy in copies[:-1]:
         copy.wait()
     live = counts[0]
     slot = lax.broadcasted_iota(jnp.int32, places.shape, 1)
     places[...] = jnp.where(slot < live, places[...], -1)
     for s in range(SLOTS):
         high[s], low[s] = split(tiles[s])
+    copies[-1].wait()
     for s in range(SLOTS):
         row = coords[0, s]
         col = pl.multiple_of(coords[1, s] * TILE, TILE)

time: 92.7 us -> 92.7 us (level)
  no operation moved by 1% of the time
where the time goes in v7:
time: 92.7 us; the launch traced here: 92.3 us
  blocking collectives  73.4 us (79%)
  starting transfers between devices  11.7 us (13%)
  Pallas kernels  4.31 us (5%)
  between operations  1.4 us (2%)
    all_to_all x5, blocking collectives, exchange(): lax.all_to_all(value, ('row', 'col'), 0, 0, axis_index_groups=groups, til...  73.4 us
    ppermute x1, starting transfers between devices, per_device(): lax.ppermute(send, 'row', swap)  6.59 us
    ppermute x1, starting transfers between devices, per_device(): other = lax.ppermute(mine, 'row', swap)  5.08 us
    pallas_call x1, Pallas kernels, per_device(): pl.pallas_call(forward_kernel, out_shape=[jax.ShapeDtypeStruct((RT, K, TI...  2.2 us
  transfers between devices with their start and end apart: 2, of which 2 were waited for; matrix products, arithmetic and copies ran while one was open for 1% of the time, Pallas kernels for 1%

profile of v7, /device:TPU:1, one launch (start us, length us, event | category | flops | bytes accessed | tf_op | source)
XLA Modules:
  0.0 92.3 jit_solution(16198462556752015095)
XLA Ops:
  1.3 2.2 %forward.1 = (f32[16,32,128]{2,1,0:T(8,128)S(1)}, bf16[16,128,128]{2,1,0:T(8,128)(2,1)S(1)}, bf16[16,128,128]{2,1,0:T(8,128)(2,1)S(1)}, s32[2,16]{1,0:T(2,128)S(1)}) custom-call(s32[1]{0:T(128)} %bitcast.7.counts_in, s32[2,16]{1,0:T(2,128)} %bitcast.12, f32[16,128,128]{2,1,0:T(8,128)} %bitcast.10, f32[32,4096]{1,0:T(8,128)} %basis_in.1), custom_call_target="tpu_custom_call" | custom-call | flops 16777216 | bytes 1900000 | tf_op jit(solution)/shard_map/forward/pallas_call | solution.py:188
  3.5 15.3 %all_to_all.32.parts = f32[16,32,128]{2,1,0:T(8,128)S(1)} all-to-all(f32[16,32,128]{2,1,0:T(8,128)S(1)} %get-tuple-element.20), channel_id=1, replica_groups={{66,65,64,67,34,33,32,35,98,97,96,99,2,1,0,3},{70,69,68,71,38,37,36,39,..., dimensions={0} | all-to-all | bytes 524288 | tf_op jit(solution)/shard_map/image_near_sum/all_to_all | solution.py:61
  18.8 28.3 %all_to_all.33.parts = f32[8,32,128]{2,1,0:T(8,128)S(1)} all-to-all(f32[8,32,128]{2,1,0:T(8,128)S(1)} %image_near_sum.1), channel_id=1, replica_groups={{24,28,20,16,8,12,4,0},{25,29,21,17,9,13,5,1},{26,30,22,18,10,14,6,2},{..., dimensions={0} | all-to-all | bytes 262144 | tf_op jit(solution)/shard_map/image_far_sum/all_to_all | solution.py:61
  47.2 12.0 %all_to_all.34.image = f32[16,32,128]{2,1,0:T(8,128)S(1)} all-to-all(f32[16,32,128]{2,1,0:T(8,128)S(1)} %image_far_sum.1), channel_id=1, replica_groups={{66,65,64,67,34,33,32,35,98,97,96,99,2,1,0,3},{70,69,68,71,38,37,36,39,..., dimensions={0} | all-to-all | bytes 524288 | tf_op jit(solution)/shard_map/image_gather/all_to_all | solution.py:61
  59.2 0.5 backward.1
  59.8 6.6 %collective-permute-start = (f32[32,2048]{1,0:T(8,128)S(1)}, f32[32,2048]{1,0:T(8,128)S(1)}, u32[]{:S(2)}, u32[]{:S(2)}) collective-permute-start(f32[32,2048]{1,0:T(8,128)S(1)} %get-tuple-element.21), channel_id=1, source_target_pairs={{0,128},{128,0},{256,384},{384,256},{512,640},{640,512},{768,896},... | collective-permute-start | bytes 786440 | tf_op jit(solution)/shard_map/back_core_sum/ppermute | solution.py:235
  66.4 0.1 constant_dynamic-slice_fusion
  66.5 0.7 copy.7
  67.2 0.4 collective-permute-done
  67.6 9.3 %all_to_all.35.parts = f32[4,8,2048]{2,1,0:T(8,128)S(1)} all-to-all(f32[4,8,2048]{2,1,0:T(8,128)S(1)} %add_bitcast_fusion), channel_id=1, replica_groups={{512,256,0,768},{513,257,1,769},{514,258,2,770},{515,259,3,771},{516,26..., dimensions={0} | all-to-all | bytes 524288 | tf_op jit(solution)/shard_map/back_row_sum/all_to_all | solution.py:61
  76.9 8.5 %all_to_all.36 = f32[4,8,2048]{2,1,0:T(8,128)S(1)} all-to-all(f32[4,8,2048]{2,1,0:T(8,128)S(1)} %back_row_sum.1), channel_id=1, replica_groups={{512,256,0,768},{513,257,1,769},{514,258,2,770},{515,259,3,771},{516,26..., dimensions={0} | all-to-all | bytes 524288 | tf_op jit(solution)/shard_map/back_row_gather/all_to_all | solution.py:61
  85.3 5.1 %collective-permute-start.1 = (f32[32,2048]{1,0:T(8,128)S(1)}, f32[32,2048]{1,0:T(8,128)S(1)}, u32[]{:S(2)}, u32[]{:S(2)}) collective-permute-start(f32[32,2048]{1,0:T(8,128)S(1)} %bitcast.8), channel_id=1, source_target_pairs={{0,128},{128,0},{256,384},{384,256},{512,640},{640,512},{768,896},... | collective-permute-start | bytes 786440 | tf_op jit(solution)/shard_map/back_core_gather/ppermute | solution.py:243
  90.4 0.7 back_core_gather.2.refs_0_
  91.2 0.4 collective-permute-done.1.part
  91.6 0.7 back_core_gather.3
  (6 shorter events, 0.1 us)
Async XLA Ops:
  59.8 7.7 %collective-permute-start = (f32[32,2048]{1,0:T(8,128)S(1)}, f32[32,2048]{1,0:T(8,128)S(1)}, u32[]{:S(2)}, u32[]{:S(2)}) collective-permute-start(f32[32,2048]{1,0:T(8,128)S(1)} %get-tuple-element.21), channel_id=1, source_target_pairs={{0,128},{128,0},{256,384},{384,256},{512,640},{640,512},{768,896},... | collective-permute-start | bytes 786440 | tf_op jit(solution)/shard_map/back_core_sum/ppermute | solution.py:235
  85.3 6.2 %collective-permute-start.1 = (f32[32,2048]{1,0:T(8,128)S(1)}, f32[32,2048]{1,0:T(8,128)S(1)}, u32[]{:S(2)}, u32[]{:S(2)}) collective-permute-start(f32[32,2048]{1,0:T(8,128)S(1)} %bitcast.8), channel_id=1, source_target_pairs={{0,128},{128,0},{256,384},{384,256},{512,640},{640,512},{768,896},... | collective-permute-start | bytes 786440 | tf_op jit(solution)/shard_map/back_core_gather/ppermute | solution.py:243
